TPU v7x, 32 devices: a whole 2x2x4 slice. The times are simulated.
32 devices in a mesh: section: 4 (over y, x), band: 8 (over z, core).
Axes of the slice: x: 2, y: 2, z: 4, core: 2. Of those that a mesh axis runs over, the one named last changes fastest.
Arguments:
- control: bfloat16 [4, 512, 2, 128, 512], P('section', 'band'), may hold values from -6 to 6
- legendre: bfloat16 [512, 512, 512], P('band'), may hold values from -0.25 to 0.25
- spectral_sd: float32 [4, 512], P('section'), may hold values from 0.3 to 3
- vertical: bfloat16 [4, 128, 128], P('section'), may hold values from -0.5 to 0.5
- obs_lon: int32 [512, 1024], P('band'), may hold values from 0 to 1023
- obs_count: int32 [512], P('band'), may hold values from 1 to 1024, as said below
- kernels: bfloat16 [512, 1024, 128], P('band'), may hold values from 0 to 0.0039978027
- obs_value: float32 [512, 1024], P('band'), may hold values from -8 to 8
- obs_weight: float32 [512, 1024], P('band'), may hold values from 1 to 16
Outputs:
- gradient: bfloat16 [4, 512, 2, 128, 512], P('section', 'band')
- departures: float32 [512, 1024], P('band')
Inputs may be any that keep to these rules, and one draw needn't show every extreme that they name: Slots 0 to obs_count - 1 of a latitude row hold its soundings, the others are empty; some row holds exactly 1024.
All inputs are finite; a program needn't handle non-finite values.
Results may differ from a plain program's by a relative error of at most 0.014.
Values may be sent and summed in bfloat16 or wider, within the bound.
A program may use at most 192 MiB of HBM per device.

v0:
```python
import math

import jax
import jax.numpy as jnp
from jax import lax
from jax.sharding import PartitionSpec as P

M = 512
NLON = 1024


def make_basis(longitude):
    wave_ids = jnp.arange(M, dtype=jnp.int32)
    phase_idx = longitude[..., None] * wave_ids % NLON
    angles = phase_idx.astype(jnp.float32) * (2.0 * math.pi / NLON)
    wave_weight = jnp.where(wave_ids == 0, 1.0, 2.0).astype(jnp.float32)
    fourier = jnp.stack([wave_weight * jnp.cos(angles), -wave_weight * jnp.sin(angles)], axis=-2)
    return fourier.astype(jnp.bfloat16)


def observe(evolved, fourier, counts, kern_rows, value_rows, weight_rows):
    slot_ids = lax.broadcasted_iota(jnp.int32, evolved.shape, 1)
    is_live = slot_ids < counts[:, None]
    departures = jnp.where(is_live, evolved - value_rows, jnp.float32(0.0))
    adjoint_columns = (
        (weight_rows * departures)[:, :, None] * kern_rows.astype(jnp.float32)
    ).astype(jnp.bfloat16)
    adjoint_fields = jnp.einsum(
        "jqrm,jql->mjrl", fourier, adjoint_columns, preferred_element_type=jnp.float32
    )
    return (departures, adjoint_fields.astype(jnp.bfloat16))


def local(
    control, legendre, spectral_sd, vertical, obs_lon, obs_count, kernels, obs_value, obs_weight
):
    coeffs = control[0]
    spread = spectral_sd[0]
    mixing = vertical[0]
    scaled = (coeffs.astype(jnp.float32) * spread).astype(jnp.bfloat16)
    spectral_rows = jnp.einsum(
        "mnj,mrkn->mjrk", legendre, scaled, preferred_element_type=jnp.float32
    ).astype(jnp.bfloat16)
    fields = jnp.einsum(
        "mjrk,lk->mjrl", spectral_rows, mixing, preferred_element_type=jnp.float32
    ).astype(jnp.bfloat16)
    local_rows = obs_lon.shape[0]
    wave_local = fields.shape[0]
    level_count = fields.shape[3]
    section_count = lax.axis_size("section")
    band_count = lax.axis_size("band")
    row_share = local_rows // section_count
    first_row = lax.axis_index("section") * row_share
    stacked = fields.astype(jnp.float32).reshape(wave_local, band_count, local_rows, 2, level_count)
    summed = lax.psum_scatter(
        stacked.astype(jnp.bfloat16), "section", scatter_dimension=2, tiled=True
    ).astype(jnp.float32)
    summed_high = summed.astype(jnp.bfloat16)
    summed_low = (summed - summed_high.astype(jnp.float32)).astype(jnp.bfloat16)
    own_lon = lax.dynamic_slice_in_dim(obs_lon, first_row, row_share, 0)
    own_count = lax.dynamic_slice_in_dim(obs_count, first_row, row_share, 0)
    own_kernels = lax.dynamic_slice_in_dim(kernels, first_row, row_share, 0)
    own_value = lax.dynamic_slice_in_dim(obs_value, first_row, row_share, 0)
    own_weight = lax.dynamic_slice_in_dim(obs_weight, first_row, row_share, 0)
    fourier = make_basis(own_lon)
    high_part = jnp.einsum(
        "jqrm,mjrl->jql",
        fourier,
        lax.all_to_all(summed_high, "band", split_axis=1, concat_axis=0, tiled=True)[:, 0],
        preferred_element_type=jnp.float32,
    )
    low_part = jnp.einsum(
        "jqrm,mjrl->jql",
        fourier,
        lax.all_to_all(summed_low, "band", split_axis=1, concat_axis=0, tiled=True)[:, 0],
        preferred_element_type=jnp.float32,
    )
    columns = high_part + low_part
    evolved = jnp.sum(own_kernels.astype(jnp.float32) * columns, axis=2)
    own_departures, own_adjoint = observe(
        evolved, fourier, own_count, own_kernels, own_value, own_weight
    )
    departures = lax.all_gather(own_departures, "section", axis=0, tiled=True)
    returned = lax.all_to_all(own_adjoint[:, None], "band", split_axis=0, concat_axis=1, tiled=True)
    gathered = lax.all_gather(returned, "section", axis=2, tiled=True)
    adjoint_all = gathered.reshape(wave_local, band_count * local_rows, 2, level_count)
    back_rows = jnp.einsum(
        "mjrl,lk->mjrk", adjoint_all, mixing, preferred_element_type=jnp.float32
    ).astype(jnp.bfloat16)
    gradient_terms = jnp.einsum(
        "mjrk,mnj->mrkn", back_rows, legendre, preferred_element_type=jnp.float32
    )
    gradient = (coeffs.astype(jnp.float32) + spread * gradient_terms).astype(jnp.bfloat16)
    return (gradient[None], departures)


def solution(mesh):
    in_specs = (
        P("section", "band", None, None, None),
        P("band", None, None),
        P("section", None),
        P("section", None, None),
        P("band", None),
        P("band"),
        P("band", None, None),
        P("band", None),
        P("band", None),
    )
    out_specs = (P("section", "band", None, None, None), P("band", None))
    return jax.shard_map(local, mesh=mesh, in_specs=in_specs, out_specs=out_specs, check_vma=False)
```

profile of v0, /device:TPU:0, one launch (start us, length us, event | category | flops | bytes accessed | tf_op | source)
XLA Modules:
  0.0 828.4 jit_solution(13035662435349738152)
XLA Ops:
  7.2 24.8 %fusion.30 = bf16[64,512,2,128]{3,1,2,0:T(8,128)(2,1)} fusion(bf16[64,512,512]{2,1,0:T(8,128)(2,1)} %param.10, bf16[1,64,2,128,512]{4,3,2,1,0:T(8,128)(2,1)} %param.9, f32[512]{0:T(512)} %bitcast.91, bf16[1,128,128]{2,1,0:T(8,128)(2,1)} %param.12), kind=kOutput, calls=%fused_computation.30 | convolution fusion | flops 10779361280 | bytes 67143680 | tf_op jit(solution)/shard_map/mjrk,lk->mjrl/dot_general | solution.py:44
  32.0 14.4 %copy.22 = bf16[64,8,64,2,128]{4,2,3,0,1:T(8,128)(2,1)} copy(bf16[64,8,64,2,128]{4,2,1,3,0:T(8,128)(2,1)} %bitcast.89) | data formatting | bytes 33554432 | tf_op jit(solution)/shard_map/convert_element_type | solution.py:56
  46.4 156.7 %reduce-scatter.2.cloned.1.call-done = bf16[64,8,16,2,128]{4,2,3,0,1:T(8,128)(2,1)} async-done(((bf16[64,8,64,2,128]{4,2,3,0,1:T(8,128)(2,1)}), bf16[64,8,16,2,128]{4,2,3,0,1:T(8,128)(2,1)}) %reduce-scatter.2.cloned.1.call-update) | async-done | bytes 4194320 | tf_op jit(solution)/shard_map/reduce_scatter | solution.py:55
  203.1 5.1 subtract_convert_fusion
  208.2 4.6 all-to-all-start.1
  212.8 0.1 dynamic_slice.16
  212.9 4.6 constant_dynamic-slice_fusion.1
  217.5 6.3 copy.36
  223.9 83.1 %all-to-all-done.1 = bf16[64,8,16,2,128]{4,2,3,0,1:T(8,128)(2,1)} async-done(((bf16[64,8,16,2,128]{4,2,3,0,1:T(8,128)(2,1)}), bf16[64,8,16,2,128]{4,2,3,0,1:T(8,128)(2,1)}, u32[]{:S(2)}, u32[]{:S(2)}) %all-to-all-start.1) | async-done | bytes 4194336 | tf_op jit(solution)/shard_map/all_to_all | solution.py:75
  306.9 4.6 all-to-all-start
  311.5 0.2 all-gather.3.cloned.1.call-start
  311.7 141.2 %multiply_convert_fusion.1 = (bf16[16,1024,1,512]{3,1,2,0:T(8,128)(2,1)}, bf16[16,1024,1,512]{3,1,2,0:T(8,128)(2,1)}) fusion(s32[16,1024]{1,0:T(8,128)S(1)} %constant_dynamic-slice_fusion, f32[512]{0:T(512)S(1)} %get-tuple-element.6, f32[512]{0:T(512)S(1)} %get-tuple-element.7), kind=kLoop, calls=%fused_computation.16 | loop fusion | flops 150994944 | bytes 33624064 | tf_op jit(solution)/shard_map/convert.1
  453.0 20.1 %fusion.38 = f32[16,1024,128,1]{1,2,3,0:T(8,128)} fusion(bf16[16,1024,1,512]{3,1,2,0:T(8,128)(2,1)} %get-tuple-element.5, bf16[16,1024,1,512]{3,1,2,0:T(8,128)(2,1)} %get-tuple-element.4, bf16[512,16,2,128]{3,1,2,0:T(8,128)(2,1)} %bitcast.17), kind=kOutput, calls=%fused_computation.32 | convolution fusion | flops 4311744512 | bytes 46137344 | tf_op jit(solution)/shard_map/jqrm,mjrl->jql/dot_general | solution.py:72
  473.1 20.0 %fusion.44 = f32[16,1024]{1,0:T(8,128)S(1)} fusion(bf16[16,1024,128]{1,2,0:T(8,128)(2,1)} %copy.36, f32[16,1024,128,1]{1,2,3,0:T(8,128)} %fusion.38, bf16[512,16,2,128]{3,1,2,0:T(8,128)(2,1)} %bitcast.12, bf16[16,1024,1,512]{3,1,2,0:T(8,128)(2,1)} %get-tuple-element.5, bf16[16,1024,1,512]{3,1,2,0:T(8,128)(2,1)} %get-tuple-element.4), kind=kOutput, calls=%fused_computation.34 | convolution fusion | flops 4320116736 | bytes 50397184 | tf_op jit(solution)/shard_map/jqrm,mjrl->jql/dot_general | solution.py:66
  493.1 1.0 dynamic-slice_multiply_fusion
  494.1 15.4 %convert_bitcast_fusion = bf16[512,1,16,2,128]{0,4,3,2,1:T(8,128)(2,1)} fusion(bf16[16,1024,1,512]{3,1,2,0:T(8,128)(2,1)} %get-tuple-element.5, bf16[16,1024,1,512]{3,1,2,0:T(8,128)(2,1)} %get-tuple-element.4, bf16[16,1024,128]{1,2,0:T(8,128)(2,1)} %copy.36, f32[16,1024]{1,0:T(8,128)S(1)} %get-tuple-element.2), kind=kOutput, calls=%fused_computation.41 | convolution fusion | flops 4370464768 | bytes 42008576 | tf_op jit(solution)/shard_map/jqrm,jql->mjrl/dot_general | solution.py:28
  509.5 11.1 %copy.25 = bf16[512,1,16,2,128]{4,3,2,1,0:T(2,128)(2,1)} copy(bf16[512,1,16,2,128]{0,4,3,2,1:T(8,128)(2,1)} %convert_bitcast_fusion) | data formatting | bytes 8388608 | tf_op jit(solution)/shard_map/broadcast_in_dim | solution.py:84
  520.6 98.8 %all_to_all.48 = bf16[512,1,16,2,128]{4,3,2,1,0:T(2,128)(2,1)S(1)} all-to-all(bf16[512,1,16,2,128]{4,3,2,1,0:T(2,128)(2,1)} %copy.25), channel_id=1, replica_groups=mesh['section'=4,'band'=8] {'band'}, dimensions={0} | all-to-all | bytes 8388608 | tf_op jit(solution)/shard_map/all_to_all | solution.py:84
  619.4 2.6 copy.26
  622.0 9.0 %all_gather.7 = f32[64,1024]{1,0:T(8,128)S(1)} all-gather(f32[16,1024]{1,0:T(8,128)S(1)} %get-tuple-element.3), channel_id=1, replica_groups=mesh['section'=4,'band'=8] {'section'}, dimensions={0}, use_global_device_ids=true | all-gather | bytes 327680 | tf_op jit(solution)/shard_map/all_gather | solution.py:83
  631.0 146.3 %all-gather.3.cloned.1.call-done = bf16[64,8,1,64,2,128]{5,3,4,2,0,1:T(8,128)(2,1)} async-done(((bf16[64,8,1,16,2,128]{5,3,4,2,0,1:T(8,128)(2,1)}), bf16[64,8,1,64,2,128]{5,3,4,2,0,1:T(8,128)(2,1)}) %all-gather.3.cloned.1.call-update) | async-done | bytes 16777232 | tf_op jit(solution)/shard_map/all_gather | solution.py:85
  777.3 14.1 %copy.27 = bf16[64,8,1,64,2,128]{5,3,1,4,0,2:T(8,128)(2,1)} copy(bf16[64,8,1,64,2,128]{5,3,4,2,0,1:T(8,128)(2,1)} %all-gather.3.cloned.1.call-done) | data formatting | bytes 33554432 | tf_op jit(solution)/shard_map/all_gather | solution.py:85
  791.4 29.5 %fusion.12 = bf16[1,64,2,128,512]{4,3,2,1,0:T(8,128)(2,1)} fusion(bf16[1,64,2,128,512]{4,3,2,1,0:T(8,128)(2,1)} %param.9, f32[512]{0:T(512)S(1)} %bitcast.92, bf16[64,512,512]{2,1,0:T(8,128)(2,1)} %param.10, bf16[64,512,2,128]{3,1,2,0:T(8,128)(2,1)} %bitcast.88, bf16[1,128,128]{2,1,0:T(8,128)(2,1)S(1)} %copy-done.2), kind=kOutput, calls=%fused_computation.20 | convolution fusion | flops 10779361280 | bytes 83920896 | tf_op jit(solution)/shard_map/mjrk,mnj->mrkn/dot_general | solution.py:90
  820.9 0.7 copy.44
  (16 shorter events, 0.1 us)
Async XLA Ops:
  7.2 216.7 %copy-start = (s32[64,1024]{1,0:T(8,128)S(1)}, s32[64,1024]{1,0:T(8,128)}, u32[]{:S(2)}) copy-start(s32[64,1024]{1,0:T(8,128)} %param.13) | copy-start | bytes 786436
  7.2 195.9 %reduce-scatter.2.cloned.1.call-start = ((), (), s32[]{:S(2)}) async-start(), calls=%async_computation.4 | async-start | bytes 20971520 | tf_op jit(solution)/shard_map/reduce_scatter | solution.py:55
  46.4 166.4 %copy-start.4 = (s32[64]{0:T(128)S(1)}, s32[64]{0:T(128)}, u32[]{:S(2)}) copy-start(s32[64]{0:T(128)} %param.14) | copy-start | bytes 772
  208.2 98.7 %all-to-all-start.1 = ((bf16[64,8,16,2,128]{4,2,3,0,1:T(8,128)(2,1)}), bf16[64,8,16,2,128]{4,2,3,0,1:T(8,128)(2,1)}, u32[]{:S(2)}, u32[]{:S(2)}) async-start(bf16[64,8,16,2,128]{4,2,3,0,1:T(8,128)(2,1)} %subtract_convert_fusion), calls=%async_computation.2 | async-start | bytes 8388608 | tf_op jit(solution)/shard_map/all_to_all | solution.py:75
  306.9 166.2 %all-to-all-start = ((bf16[64,8,16,2,128]{4,2,3,0,1:T(8,128)(2,1)}), bf16[64,8,16,2,128]{4,2,3,0,1:T(8,128)(2,1)}, u32[]{:S(2)}, u32[]{:S(2)}) async-start(bf16[64,8,16,2,128]{4,2,3,0,1:T(8,128)(2,1)} %reduce-scatter.2.cloned.1.call-done), calls=%async_computation.1 | async-start | bytes 8388608 | tf_op jit(solution)/shard_map/all_to_all | solution.py:69
  311.5 465.8 %all-gather.3.cloned.1.call-start = ((), (), s32[]{:S(2)}) async-start(), calls=%async_computation.5 | async-start | bytes 20971520 | tf_op jit(solution)/shard_map/all_gather | solution.py:85
  631.0 160.4 %copy-start.2 = (bf16[1,128,128]{2,1,0:T(8,128)(2,1)S(1)}, bf16[1,128,128]{2,1,0:T(8,128)(2,1)}, u32[]{:S(2)}) copy-start(bf16[1,128,128]{2,1,0:T(8,128)(2,1)} %param.12) | copy-start | bytes 98308
  631.0 160.4 %copy-start.3 = (f32[1,512]{1,0:T(1,128)S(1)}, f32[1,512]{1,0:T(1,128)}, u32[]{:S(2)}) copy-start(f32[1,512]{1,0:T(1,128)} %param.11) | copy-start | bytes 6148
  791.4 30.2 %copy-start.1 = (s32[64,1024]{1,0:T(8,128)S(1)}, s32[64,1024]{1,0:T(8,128)}, u32[]{:S(2)}) copy-start(s32[64,1024]{1,0:T(8,128)} %param.13) | copy-start | bytes 786436
Sparse Core Ops, SparseCore 0:
  46.5 156.4 reduce-scatter.1
  622.1 155.1 all-gather.2
where the time goes:
time: 829 us; the launch traced here: 828 us
  waiting for transfers between devices  386 us (47%)
  other arithmetic  147 us (18%)
  matrix products  110 us (13%)
  blocking collectives  108 us (13%)
  local copies, waits for them, and re-layouts  53.9 us (7%)
  between operations  14.1 us (2%)
  starting transfers between devices  9.41 us (1%)
    reduce_scatter x1, waiting for transfers between devices, local(): lax.psum_scatter(stacked.astype(jnp.bfloat16), 'section', scatter_dimensi...  157 us
    all_gather x1, waiting for transfers between devices, local(): gathered = lax.all_gather(returned, 'section', axis=2, tiled=True)  146 us
    another operation x1, other arithmetic  141 us
    all_to_all x1, blocking collectives, local(): lax.all_to_all(own_adjoint[:, None], 'band', split_axis=0, concat_axis=1,...  98.8 us
    all_to_all x1, waiting for transfers between devices, local(): lax.all_to_all(summed_low, 'band', split_axis=1, concat_axis=0, tiled=True)  83.1 us
    dot_general x1, matrix products, local(): jnp.einsum('mjrk,mnj->mrkn', back_rows, legendre, preferred_element_type=...  29.5 us
    dot_general x1, matrix products, local(): jnp.einsum('mjrk,lk->mjrl', spectral_rows, mixing, preferred_element_type...  24.8 us
    dot_general x1, matrix products, local(): jnp.einsum('jqrm,mjrl->jql', fourier, lax.all_to_all(summed_low, 'band',...  20.1 us
  transfers between devices with their start and end apart: 4, of which 3 were waited for; matrix products, arithmetic and copies ran while one was open for 21% of the time, Pallas kernels for 0%

commit v1 on v0

v1 whole, which is shorter than its diff:
```python
import math

import jax
import jax.numpy as jnp
from jax import lax
from jax.sharding import PartitionSpec as P

NLON = 1024
CHUNKS = 4


def make_basis(longitude, wave_ids):
    waves = wave_ids.astype(jnp.float32)
    quarter = lax.broadcasted_iota(jnp.int32, (2, 1), 0).astype(jnp.float32) * 0.25
    turns = (longitude.astype(jnp.float32) * (1.0 / NLON))[..., None, None] * waves + quarter
    frac = turns - jnp.round(turns)
    x = 0.25 - jnp.abs(frac)
    z = x * x
    two_pi = 2.0 * math.pi
    coefs = [((-1) ** i) * two_pi ** (2 * i + 1) / math.factorial(2 * i + 1) for i in range(7)]
    acc = jnp.float32(coefs[-1])
    for coef in coefs[-2::-1]:
        acc = acc * z + jnp.float32(coef)
    weight = jnp.where(wave_ids == 0, 1.0, 2.0).astype(jnp.float32)
    return (acc * (x * weight)).astype(jnp.bfloat16)


def local(
    control, legendre, spectral_sd, vertical, obs_lon, obs_count, kernels, obs_value, obs_weight
):
    coeffs = control[0]
    spread = spectral_sd[0]
    mixing = vertical[0]
    local_rows = obs_lon.shape[0]
    wave_local, _, level_count, _ = coeffs.shape
    row_count = legendre.shape[2]
    section_count = lax.axis_size("section")
    band_count = lax.axis_size("band")
    row_share = local_rows // section_count
    first_row = lax.axis_index("section") * row_share
    chunks = math.gcd(CHUNKS, wave_local)
    step = wave_local // chunks

    own_lon = lax.dynamic_slice_in_dim(obs_lon, first_row, row_share, 0)
    own_count = lax.dynamic_slice_in_dim(obs_count, first_row, row_share, 0)
    own_kernels = lax.dynamic_slice_in_dim(kernels, first_row, row_share, 0)
    own_value = lax.dynamic_slice_in_dim(obs_value, first_row, row_share, 0)
    own_weight = lax.dynamic_slice_in_dim(obs_weight, first_row, row_share, 0)

    columns = 0.0
    bases = []
    for i in range(chunks):
        part = slice(i * step, (i + 1) * step)
        scaled = (coeffs[part].astype(jnp.float32) * spread).astype(jnp.bfloat16)
        spectral_rows = jnp.einsum(
            "mnj,mrkn->mjrk", legendre[part], scaled, preferred_element_type=jnp.float32
        ).astype(jnp.bfloat16)
        fields = jnp.einsum(
            "mjrk,lk->mjrl", spectral_rows, mixing, preferred_element_type=jnp.float32
        ).astype(jnp.bfloat16)
        stacked = fields.reshape(step, band_count, local_rows, 2, level_count)
        summed = lax.psum_scatter(stacked, "section", scatter_dimension=2, tiled=True)
        moved = lax.all_to_all(summed, "band", split_axis=1, concat_axis=0, tiled=True)[:, 0]
        wave_ids = (
            jnp.arange(band_count, dtype=jnp.int32)[:, None] * wave_local
            + i * step
            + jnp.arange(step, dtype=jnp.int32)
        ).reshape(-1)
        basis = make_basis(own_lon, wave_ids)
        bases.append(basis)
        columns = columns + jnp.einsum(
            "jqrm,mjrl->jql", basis, moved, preferred_element_type=jnp.float32
        )
    wide_kernels = own_kernels.astype(jnp.float32)
    evolved = jnp.sum(wide_kernels * columns, axis=2)
    slot_ids = lax.broadcasted_iota(jnp.int32, evolved.shape, 1)
    is_live = slot_ids < own_count[:, None]
    own_departures = jnp.where(is_live, evolved - own_value, jnp.float32(0.0))
    adjoint_columns = ((own_weight * own_departures)[:, :, None] * wide_kernels).astype(jnp.bfloat16)

    pieces = []
    for i in range(chunks):
        part = slice(i * step, (i + 1) * step)
        own_adjoint = jnp.einsum(
            "jqrm,jql->mjrl", bases[i], adjoint_columns, preferred_element_type=jnp.float32
        ).astype(jnp.bfloat16)
        returned = lax.all_to_all(
            own_adjoint[:, None], "band", split_axis=0, concat_axis=1, tiled=True
        )
        gathered = lax.all_gather(returned, "section", axis=2, tiled=True)
        adjoint_all = gathered.reshape(step, row_count, 2, level_count)
        back_rows = jnp.einsum(
            "mjrl,lk->mjrk", adjoint_all, mixing, preferred_element_type=jnp.float32
        ).astype(jnp.bfloat16)
        gradient_terms = jnp.einsum(
            "mjrk,mnj->mrkn", back_rows, legendre[part], preferred_element_type=jnp.float32
        )
        pieces.append(
            (coeffs[part].astype(jnp.float32) + spread * gradient_terms).astype(jnp.bfloat16)
        )
    departures = lax.all_gather(own_departures, "section", axis=0, tiled=True)
    return (jnp.concatenate(pieces, axis=0)[None], departures)


def solution(mesh):
    in_specs = (
        P("section", "band", None, None, None),
        P("band", None, None),
        P("section", None),
        P("section", None, None),
        P("band", None),
        P("band"),
        P("band", None, None),
        P("band", None),
        P("band", None),
    )
    out_specs = (P("section", "band", None, None, None), P("band", None))
    return jax.shard_map(local, mesh=mesh, in_specs=in_specs, out_specs=out_specs, check_vma=False)
```

time: 829 us -> 604 us (0.73); the launches traced: 828 us -> 594 us
  waiting for transfers between devices: 386 us -> 131 us
  other arithmetic: 147 us -> 28.1 us
  matrix products: 110 us -> 195 us
  starting transfers between devices: 9.41 us -> 30.7 us
  blocking collectives: 108 us -> 127 us
  local copies, waits for them, and re-layouts: 53.9 us -> 67.3 us
    another operation x1 -> x0, other arithmetic: 141 us -> none
    all_gather x1 -> x4, waiting for transfers between devices: 146 us -> 21.1 us  [local(): gathered = lax.all_gather(returned, 'section', axis=2, tiled=True)]
    dot_general x4 -> x12, matrix products: 85 us -> 162 us  [the longest x4 65.5 us: local(): jnp.einsum('jqrm,mjrl->jql', basis, moved, preferred_element_type=jnp.flo...]
    all_to_all x2 -> x4, waiting for transfers between devices: 83.1 us -> 10.8 us  [local(): lax.all_to_all(summed, 'band', split_axis=1, concat_axis=0, tiled=True)]
    reduce_scatter x1 -> x4, waiting for transfers between devices: 157 us -> 99.2 us  [local(): lax.psum_scatter(stacked, 'section', scatter_dimension=2, tiled=True)]
    reshape x0 -> x4, local copies, waits for them, and re-layouts: none -> 23.1 us  [local(): stacked = fields.reshape(step, band_count, local_rows, 2, level_count)]
    all_to_all x2 -> x4, starting transfers between devices: 9.15 us -> 30 us  [local(): lax.all_to_all(summed, 'band', split_axis=1, concat_axis=0, tiled=True)]
    all_to_all x1 -> x4, blocking collectives: 98.8 us -> 116 us  [local(): lax.all_to_all(own_adjoint[:, None], 'band', split_axis=0, concat_axis=1,...]
  transfers between devices with their start and end apart: 4 -> 12, of which waited for: 3 -> 7; matrix products, arithmetic and copies ran while one was open for 21% -> 35% of each run, Pallas kernels for 0% -> 0%
where the time goes in v1:
time: 604 us; the launch traced here: 594 us
  matrix products  195 us (32%)
  waiting for transfers between devices  131 us (22%)
  blocking collectives  127 us (21%)
  local copies, waits for them, and re-layouts  67.3 us (11%)
  starting transfers between devices  30.7 us (5%)
  other arithmetic  28.1 us (5%)
  between operations  14.5 us (2%)
    all_to_all x4, blocking collectives, local(): lax.all_to_all(own_adjoint[:, None], 'band', split_axis=0, concat_axis=1,...  116 us
    reduce_scatter x4, waiting for transfers between devices, local(): lax.psum_scatter(stacked, 'section', scatter_dimension=2, tiled=True)  99.2 us
    dot_general x4, matrix products, local(): jnp.einsum('jqrm,mjrl->jql', basis, moved, preferred_element_type=jnp.flo...  65.5 us
    dot_general x4, matrix products, local(): jnp.einsum('jqrm,jql->mjrl', bases[i], adjoint_columns, preferred_element...  58.7 us
    dot_general x4, matrix products, local(): jnp.einsum('mjrk,mnj->mrkn', back_rows, legendre[part], preferred_element...  38.2 us
    dot_general x4, matrix products, local(): jnp.einsum('mjrk,lk->mjrl', spectral_rows, mixing, preferred_element_type...  33.1 us
    all_to_all x4, starting transfers between devices, local(): lax.all_to_all(summed, 'band', split_axis=1, concat_axis=0, tiled=True)  30 us
    reshape x4, local copies, waits for them, and re-layouts, local(): stacked = fields.reshape(step, band_count, local_rows, 2, level_count)  23.1 us
  transfers between devices with their start and end apart: 12, of which 7 were waited for; matrix products, arithmetic and copies ran while one was open for 35% of the time, Pallas kernels for 0%

profile of v1, /device:TPU:0, one launch (start us, length us, event | category | flops | bytes accessed | tf_op | source)
XLA Modules:
  0.0 594.4 jit_solution(80890196604083906)
XLA Ops:
  64.8 13.5 %reduce-scatter.5.cloned.1.call-done = bf16[16,8,16,2,128]{4,2,3,0,1:T(8,128)(2,1)} async-done(((bf16[16,8,64,2,128]{4,2,3,0,1:T(8,128)(2,1)}), bf16[16,8,16,2,128]{4,2,3,0,1:T(8,128)(2,1)}) %reduce-scatter.5.cloned.1.call-update) | async-done | bytes 1048592 | tf_op jit(solution)/shard_map/reduce_scatter | solution.py:62
  78.3 16.1 %all-to-all-start = ((bf16[16,8,16,2,128]{4,2,3,0,1:T(8,128)(2,1)}), bf16[16,8,16,2,128]{4,2,3,0,1:T(8,128)(2,1)S(1)}, u32[]{:S(2)}, u32[]{:S(2)}) async-start(bf16[16,8,16,2,128]{4,2,3,0,1:T(8,128)(2,1)} %reduce-scatter.5.cloned.1.call-done), calls=%async_computation.1 | async-start | bytes 2097152 | tf_op jit(solution)/shard_map/all_to_all | solution.py:63
  107.2 11.8 %broadcast_multiply_fusion.3 = (f32[16,1024,128]{2,1,0:T(8,128)}, f32[16,1024,128]{2,1,0:T(8,128)}, f32[16,1024,128]{2,1,0:T(8,128)}, f32[16,1024,128]{2,1,0:T(8,128)}) fusion(f32[128]{0:T(128)S(1)} %convert_element_type.211, f32[16,1024]{1,0:T(8,128)S(1)} %convert_multiply_fusion.6, f32[128]{0:T(128)S(1)} %convert_element_type.219, ...), kind=kLoop, calls=%fused_computation.128 | loop fusion | flops 8388608 | bytes 33622016 | tf_op jit(solution)/shard_map/mul | solution.py:15
  118.9 15.2 %reduce-scatter.7.cloned.1.call-done = bf16[16,8,16,2,128]{4,2,3,0,1:T(8,128)(2,1)} async-done(((bf16[16,8,64,2,128]{4,2,3,0,1:T(8,128)(2,1)}), bf16[16,8,16,2,128]{4,2,3,0,1:T(8,128)(2,1)}) %reduce-scatter.7.cloned.1.call-update) | async-done | bytes 1048592 | tf_op jit(solution)/shard_map/reduce_scatter | solution.py:62
  138.8 15.8 %fusion.59 = f32[16,1024,128,1]{1,2,3,0:T(8,128)} fusion(f32[128]{0:T(128)S(1)} %select_n.54, f32[2]{0:T(128)S(1)} %convert_multiply_fusion.7, f32[16,1024,128]{2,1,0:T(8,128)} %get-tuple-element.4, bf16[128,16,2,128]{3,1,2,0:T(8,128)(2,1)S(1)} %bitcast.258), kind=kOutput, calls=%fused_computation.97 | convolution fusion | flops 1161822208 | bytes 17826312 | tf_op jit(solution)/shard_map/jqrm,mjrl->jql/dot_general | solution.py:71
  154.6 35.2 %reduce-scatter.9.cloned.1.call-done = bf16[16,8,16,2,128]{4,2,3,0,1:T(8,128)(2,1)} async-done(((bf16[16,8,64,2,128]{4,2,3,0,1:T(8,128)(2,1)}), bf16[16,8,16,2,128]{4,2,3,0,1:T(8,128)(2,1)}) %reduce-scatter.9.cloned.1.call-update) | async-done | bytes 1048592 | tf_op jit(solution)/shard_map/reduce_scatter | solution.py:62
  194.5 15.8 %fusion.61 = f32[16,1024,128,1]{1,2,3,0:T(8,128)} fusion(f32[128]{0:T(128)S(1)} %select_n.56, f32[16,1024,128]{2,1,0:T(8,128)} %get-tuple-element.5, f32[2]{0:T(128)S(1)} %convert_multiply_fusion.7, bf16[128,16,2,128]{3,1,2,0:T(8,128)(2,1)S(1)} %bitcast.260), kind=kOutput, calls=%fused_computation.99 | convolution fusion | flops 1161822208 | bytes 17826312 | tf_op jit(solution)/shard_map/jqrm,mjrl->jql/dot_general | solution.py:71
  210.3 35.3 %reduce-scatter.11.cloned.1.call-done = bf16[16,8,16,2,128]{4,2,3,0,1:T(8,128)(2,1)} async-done(((bf16[16,8,64,2,128]{4,2,3,0,1:T(8,128)(2,1)}), bf16[16,8,16,2,128]{4,2,3,0,1:T(8,128)(2,1)}) %reduce-scatter.11.cloned.1.call-update) | async-done | bytes 1048592 | tf_op jit(solution)/shard_map/reduce_scatter | solution.py:62
  250.3 15.8 %fusion.63 = f32[16,1024,128,1]{1,2,3,0:T(8,128)} fusion(f32[128]{0:T(128)S(1)} %select_n.58, f32[16,1024,128]{2,1,0:T(8,128)} %get-tuple-element.6, f32[2]{0:T(128)S(1)} %convert_multiply_fusion.7, bf16[128,16,2,128]{3,1,2,0:T(8,128)(2,1)S(1)} %bitcast.259), kind=kOutput, calls=%fused_computation.101 | convolution fusion | flops 1161822208 | bytes 17826312 | tf_op jit(solution)/shard_map/jqrm,mjrl->jql/dot_general | solution.py:71
  266.1 10.8 %all-to-all-done.3 = bf16[16,8,16,2,128]{4,2,3,0,1:T(8,128)(2,1)S(1)} async-done(((bf16[16,8,16,2,128]{4,2,3,0,1:T(8,128)(2,1)}), bf16[16,8,16,2,128]{4,2,3,0,1:T(8,128)(2,1)S(1)}, u32[]{:S(2)}, u32[]{:S(2)}) %all-to-all-start.3) | async-done | bytes 1048608 | tf_op jit(solution)/shard_map/all_to_all | solution.py:63
  276.8 18.1 %fusion.24 = f32[16,1024]{1,0:T(8,128)S(1)} fusion(bf16[16,1024,128]{1,2,0:T(8,128)(2,1)} %copy.80, f32[16,1024,128,1]{1,2,3,0:T(8,128)} %fusion.63, f32[16,1024,128,1]{1,2,3,0:T(8,128)} %fusion.61, f32[16,1024,128,1]{1,2,3,0:T(8,128)} %fusion.59, f32[128]{0:T(128)S(1)} %select_n.60, f32[16,1024,128]{2,1,0:T(8,128)} %get-tuple-element.7, ...), kind=kOutput, calls=%fused_computation.59 | convolution fusion | flops 1174388736 | bytes 38863368 | tf_op jit(solution)/shard_map/jqrm,mjrl->jql/dot_general | solution.py:71
  295.9 14.8 %fusion.188 = bf16[128,1,16,2,128]{0,4,3,2,1:T(8,128)(2,1)S(1)} fusion(f32[128]{0:T(128)S(1)} %select_n.56, f32[16,1024,128]{2,1,0:T(8,128)} %get-tuple-element.5, f32[2]{0:T(128)S(1)} %convert_multiply_fusion.7, bf16[16,1024,128]{1,2,0:T(8,128)(2,1)S(1)} %copy-done.1, f32[16,1024]{1,0:T(8,128)S(1)} %get-tuple-element.2), kind=kOutput, calls=%fused_computation.150 | convolution fusion | flops 1168637952 | bytes 13697544 | tf_op jit(solution)/shard_map/jqrm,jql->mjrl/dot_general | solution.py:84
  311.7 29.0 %all_to_all.132 = bf16[128,1,16,2,128]{4,3,2,1,0:T(2,128)(2,1)S(1)} all-to-all(bf16[128,1,16,2,128]{4,3,2,1,0:T(2,128)(2,1)S(1)} %copy.50), channel_id=1, replica_groups=mesh['section'=4,'band'=8] {'band'}, dimensions={0} | all-to-all | bytes 2097152 | tf_op jit(solution)/shard_map/all_to_all | solution.py:87
  342.1 14.6 %fusion.189 = bf16[128,1,16,2,128]{0,4,3,2,1:T(8,128)(2,1)S(1)} fusion(f32[128]{0:T(128)S(1)} %select_n.58, f32[16,1024,128]{2,1,0:T(8,128)} %get-tuple-element.6, f32[2]{0:T(128)S(1)} %convert_multiply_fusion.7, bf16[16,1024,128]{1,2,0:T(8,128)(2,1)} %copy.80, f32[16,1024]{1,0:T(8,128)S(1)} %get-tuple-element.2), kind=kOutput, calls=%fused_computation.151 | convolution fusion | flops 1168637952 | bytes 13697544 | tf_op jit(solution)/shard_map/jqrm,jql->mjrl/dot_general | solution.py:84
  357.7 29.0 %all_to_all.133 = bf16[128,1,16,2,128]{4,3,2,1,0:T(2,128)(2,1)S(1)} all-to-all(bf16[128,1,16,2,128]{4,3,2,1,0:T(2,128)(2,1)S(1)} %copy.54), channel_id=1, replica_groups=mesh['section'=4,'band'=8] {'band'}, dimensions={0} | all-to-all | bytes 2097152 | tf_op jit(solution)/shard_map/all_to_all | solution.py:87
  388.3 14.6 %fusion.190 = bf16[128,1,16,2,128]{0,4,3,2,1:T(8,128)(2,1)S(1)} fusion(f32[128]{0:T(128)S(1)} %select_n.60, f32[16,1024,128]{2,1,0:T(8,128)} %get-tuple-element.7, f32[2]{0:T(128)S(1)} %convert_multiply_fusion.7, bf16[16,1024,128]{1,2,0:T(8,128)(2,1)} %copy.80, f32[16,1024]{1,0:T(8,128)S(1)} %get-tuple-element.2), kind=kOutput, calls=%fused_computation.152 | convolution fusion | flops 1168637952 | bytes 13697544 | tf_op jit(solution)/shard_map/jqrm,jql->mjrl/dot_general | solution.py:84
  404.0 29.0 %all_to_all.134 = bf16[128,1,16,2,128]{4,3,2,1,0:T(2,128)(2,1)S(1)} all-to-all(bf16[128,1,16,2,128]{4,3,2,1,0:T(2,128)(2,1)S(1)} %copy.58), channel_id=1, replica_groups=mesh['section'=4,'band'=8] {'band'}, dimensions={0} | all-to-all | bytes 2097152 | tf_op jit(solution)/shard_map/all_to_all | solution.py:87
  434.2 14.6 %fusion.187 = bf16[128,1,16,2,128]{0,4,3,2,1:T(8,128)(2,1)S(1)} fusion(f32[128]{0:T(128)S(1)} %copy-done.3, f32[2]{0:T(128)S(1)} %convert_multiply_fusion.7, f32[16,1024,128]{2,1,0:T(8,128)} %get-tuple-element.4, bf16[16,1024,128]{1,2,0:T(8,128)(2,1)} %copy.80, f32[16,1024]{1,0:T(8,128)S(1)} %get-tuple-element.2), kind=kOutput, calls=%fused_computation.149 | convolution fusion | flops 1168637952 | bytes 13697544 | tf_op jit(solution)/shard_map/jqrm,jql->mjrl/dot_general | solution.py:84
  449.9 29.0 %all_to_all.135 = bf16[128,1,16,2,128]{4,3,2,1,0:T(2,128)(2,1)S(1)} all-to-all(bf16[128,1,16,2,128]{4,3,2,1,0:T(2,128)(2,1)S(1)} %copy.46), channel_id=1, replica_groups=mesh['section'=4,'band'=8] {'band'}, dimensions={0} | all-to-all | bytes 2097152 | tf_op jit(solution)/shard_map/all_to_all | solution.py:87
  480.1 10.9 %all_gather.19 = f32[64,1024]{1,0:T(8,128)S(1)} all-gather(f32[16,1024]{1,0:T(8,128)S(1)} %get-tuple-element.3), channel_id=1, replica_groups=mesh['section'=4,'band'=8] {'section'}, dimensions={0}, use_global_device_ids=true | all-gather | bytes 327680 | tf_op jit(solution)/shard_map/all_gather | solution.py:101
  509.1 10.4 %fusion.29 = bf16[16,2,128,512]{3,2,1,0:T(8,128)(2,1)} fusion(f32[512]{0:T(512)S(1)} %bitcast.266, bf16[1,64,2,128,512]{4,3,2,1,0:T(8,128)(2,1)} %param.9, bf16[64,512,512]{2,1,0:T(8,128)(2,1)} %param.10, bf16[16,512,2,128]{3,1,2,0:T(8,128)(2,1)} %bitcast.246, bf16[1,128,128]{2,1,0:T(8,128)(2,1)S(1)} %copy-done), kind=kOutput, calls=%fused_computation.64 | convolution fusion | flops 2694840320 | bytes 21006336 | tf_op jit(solution)/shard_map/mjrk,mnj->mrkn/dot_general | solution.py:95
  528.7 9.4 %fusion.33 = bf16[16,2,128,512]{3,2,1,0:T(8,128)(2,1)} fusion(f32[512]{0:T(512)S(1)} %bitcast.268, bf16[1,64,2,128,512]{4,3,2,1,0:T(8,128)(2,1)} %param.9, bf16[64,512,512]{2,1,0:T(8,128)(2,1)} %param.10, bf16[16,512,2,128]{3,1,2,0:T(8,128)(2,1)} %bitcast.248, bf16[1,128,128]{2,1,0:T(8,128)(2,1)S(1)} %copy-done), kind=kOutput, calls=%fused_computation.68 | convolution fusion | flops 2694840320 | bytes 21006336 | tf_op jit(solution)/shard_map/mjrk,mnj->mrkn/dot_general | solution.py:95
  538.1 19.8 %all-gather.9.cloned.1.call-done = bf16[16,8,1,64,2,128]{5,3,4,2,0,1:T(8,128)(2,1)} async-done(((bf16[16,8,1,16,2,128]{5,3,4,2,0,1:T(8,128)(2,1)}), bf16[16,8,1,64,2,128]{5,3,4,2,0,1:T(8,128)(2,1)}) %all-gather.9.cloned.1.call-update) | async-done | bytes 4194320 | tf_op jit(solution)/shard_map/all_gather | solution.py:90
  572.7 14.0 %maximum_bitcast_fusion = bf16[1,64,2,128,512]{4,3,2,1,0:T(8,128)(2,1)} fusion(bf16[16,2,128,512]{3,2,1,0:T(8,128)(2,1)} %fusion.33, bf16[16,2,128,512]{3,2,1,0:T(8,128)(2,1)} %fusion.31, bf16[16,2,128,512]{3,2,1,0:T(8,128)(2,1)} %fusion.29, bf16[16,2,128,512]{3,2,1,0:T(8,128)(2,1)} %fusion.27), kind=kLoop, calls=%fused_computation.12 | loop fusion | flops 25165824 | bytes 33554432 | tf_op jit(solution)/shard_map/broadcast_in_dim | solution.py:102
  (88 shorter events, 137.2 us)
Async XLA Ops:
  7.2 0.8 copy-start
  7.2 71.1 %reduce-scatter.5.cloned.1.call-start = ((), (), s32[]{:S(2)}) async-start(), calls=%async_computation.12 | async-start | bytes 5242880 | tf_op jit(solution)/shard_map/reduce_scatter | solution.py:62
  7.9 14.9 %copy-start.4 = (f32[1,512]{1,0:T(1,128)S(1)}, f32[1,512]{1,0:T(1,128)}, u32[]{:S(2)}) copy-start(f32[1,512]{1,0:T(1,128)} %param.11) | copy-start | bytes 6148
  22.8 111.4 %reduce-scatter.7.cloned.1.call-start = ((), (), s32[]{:S(2)}) async-start(), calls=%async_computation.13 | async-start | bytes 5242880 | tf_op jit(solution)/shard_map/reduce_scatter | solution.py:62
  36.9 153.0 %reduce-scatter.9.cloned.1.call-start = ((), (), s32[]{:S(2)}) async-start(), calls=%async_computation.14 | async-start | bytes 5242880 | tf_op jit(solution)/shard_map/reduce_scatter | solution.py:62
  50.7 44.5 %copy-start.6 = (s32[64]{0:T(128)S(1)}, s32[64]{0:T(128)}, u32[]{:S(2)}) copy-start(s32[64]{0:T(128)} %param.14) | copy-start | bytes 772
  50.7 194.9 %reduce-scatter.11.cloned.1.call-start = ((), (), s32[]{:S(2)}) async-start(), calls=%async_computation.15 | async-start | bytes 5242880 | tf_op jit(solution)/shard_map/reduce_scatter | solution.py:62
  78.3 55.9 %all-to-all-start = ((bf16[16,8,16,2,128]{4,2,3,0,1:T(8,128)(2,1)}), bf16[16,8,16,2,128]{4,2,3,0,1:T(8,128)(2,1)S(1)}, u32[]{:S(2)}, u32[]{:S(2)}) async-start(bf16[16,8,16,2,128]{4,2,3,0,1:T(8,128)(2,1)} %reduce-scatter.5.cloned.1.call-done), calls=%async_computation.1 | async-start | bytes 2097152 | tf_op jit(solution)/shard_map/all_to_all | solution.py:63
  94.6 44.2 %copy-start.2 = (f32[128]{0:T(128)}, f32[128]{0:T(128)S(1)}, u32[]{:S(2)}) copy-start(f32[128]{0:T(128)S(1)} %select_n.54) | copy-start | bytes 1540
  134.2 55.7 %all-to-all-start.1 = ((bf16[16,8,16,2,128]{4,2,3,0,1:T(8,128)(2,1)}), bf16[16,8,16,2,128]{4,2,3,0,1:T(8,128)(2,1)S(1)}, u32[]{:S(2)}, u32[]{:S(2)}) async-start(bf16[16,8,16,2,128]{4,2,3,0,1:T(8,128)(2,1)} %reduce-scatter.7.cloned.1.call-done), calls=%async_computation.3 | async-start | bytes 2097152 | tf_op jit(solution)/shard_map/all_to_all | solution.py:63
  189.9 55.7 %all-to-all-start.2 = ((bf16[16,8,16,2,128]{4,2,3,0,1:T(8,128)(2,1)}), bf16[16,8,16,2,128]{4,2,3,0,1:T(8,128)(2,1)S(1)}, u32[]{:S(2)}, u32[]{:S(2)}) async-start(bf16[16,8,16,2,128]{4,2,3,0,1:T(8,128)(2,1)} %reduce-scatter.9.cloned.1.call-done), calls=%async_computation.5 | async-start | bytes 2097152 | tf_op jit(solution)/shard_map/all_to_all | solution.py:63
  245.6 31.2 %all-to-all-start.3 = ((bf16[16,8,16,2,128]{4,2,3,0,1:T(8,128)(2,1)}), bf16[16,8,16,2,128]{4,2,3,0,1:T(8,128)(2,1)S(1)}, u32[]{:S(2)}, u32[]{:S(2)}) async-start(bf16[16,8,16,2,128]{4,2,3,0,1:T(8,128)(2,1)} %reduce-scatter.11.cloned.1.call-done), calls=%async_computation.7 | async-start | bytes 2097152 | tf_op jit(solution)/shard_map/all_to_all | solution.py:63
  250.2 240.8 %all-gather.11.cloned.1.call-start = ((), (), s32[]{:S(2)}) async-start(), calls=%async_computation.17 | async-start | bytes 5242880 | tf_op jit(solution)/shard_map/all_gather | solution.py:90
  276.8 19.1 %copy-start.1 = (bf16[16,1024,128]{1,2,0:T(8,128)(2,1)S(1)}, bf16[16,1024,128]{1,2,0:T(8,128)(2,1)}, u32[]{:S(2)}) copy-start(bf16[16,1024,128]{1,2,0:T(8,128)(2,1)} %copy.80) | copy-start | bytes 12582916
  342.0 154.6 %all-gather.13.cloned.1.call-start = ((), (), s32[]{:S(2)}) async-start(), calls=%async_computation.18 | async-start | bytes 5242880 | tf_op jit(solution)/shard_map/all_gather | solution.py:90
  387.9 46.3 %copy-start.3 = (f32[128]{0:T(128)S(1)}, f32[128]{0:T(128)}, u32[]{:S(2)}) copy-start(f32[128]{0:T(128)} %copy-done.2) | copy-start | bytes 1540
  387.9 115.6 %all-gather.15.cloned.1.call-start = ((), (), s32[]{:S(2)}) async-start(), calls=%async_computation.19 | async-start | bytes 5242880 | tf_op jit(solution)/shard_map/all_gather | solution.py:90
  434.2 123.7 %all-gather.9.cloned.1.call-start = ((), (), s32[]{:S(2)}) async-start(), calls=%async_computation.16 | async-start | bytes 5242880 | tf_op jit(solution)/shard_map/all_gather | solution.py:90
  448.9 60.2 %copy-start.5 = (f32[1,512]{1,0:T(1,128)S(1)}, f32[1,512]{1,0:T(1,128)}, u32[]{:S(2)}) copy-start(f32[1,512]{1,0:T(1,128)} %param.11) | copy-start | bytes 6148
Sparse Core Ops, SparseCore 0:
  22.9 55.3 reduce-scatter.4
  81.5 52.6 reduce-scatter.6
  137.1 52.6 reduce-scatter.8
  192.9 52.6 reduce-scatter.10
  342.1 50.4 all-gather.10
  394.3 52.5 all-gather.12
  448.8 54.6 all-gather.14
  505.3 52.5 all-gather.8

commit v2 on v1

--- a/solution.py
+++ b/solution.py
@@ -23,6 +23,59 @@
         acc = acc * z + jnp.float32(coef)
     weight = jnp.where(wave_ids == 0, 1.0, 2.0).astype(jnp.float32)
     return (acc * (x * weight)).astype(jnp.bfloat16)
+
+
+def exchange(block, bit):
+    count = lax.axis_size("section")
+    return lax.ppermute(block, "section", [(s, s ^ bit) for s in range(count)])
+
+
+def side(bit):
+    return (lax.axis_index("section") // bit) % 2
+
+
+def pick(stacked, axis, index):
+    return lax.dynamic_index_in_dim(stacked, index, axis, keepdims=False)
+
+
+def add(kept, came):
+    return (kept.astype(jnp.float32) + came.astype(jnp.float32)).astype(jnp.bfloat16)
+
+
+def sum_rows(fields, band_count, first, second):
+    step, row_count, parts, level_count = fields.shape
+    section_count = lax.axis_size("section")
+    if section_count != 4:
+        stacked = fields.reshape(step, band_count, row_count // band_count, parts, level_count)
+        return lax.psum_scatter(stacked, "section", scatter_dimension=2, tiled=True)
+    block = fields.reshape(step, band_count, 2, 2, -1, parts, level_count)
+    axis = 3 if first == 1 else 2
+    came = exchange(pick(block, axis, 1 - side(first)), first)
+    pair = add(pick(block, axis, side(first)), came)
+    came = exchange(pick(pair, 2, 1 - side(second)), second)
+    return add(pick(pair, 2, side(second)), came)
+
+
+def gather_rows(returned, first, second):
+    step, _, _, parts, level_count = returned.shape
+    section_count = lax.axis_size("section")
+    if section_count != 4:
+        gathered = lax.all_gather(returned, "section", axis=2, tiled=True)
+        return gathered.reshape(step, -1, parts, level_count), returned
+    near = exchange(returned, first)
+    far = exchange(returned, second)
+    far_near = exchange(near, second)
+    me = lax.axis_index("section")
+    all_rows = jnp.zeros((4,) + returned.shape, returned.dtype)
+    for block, flip in ((returned, 0), (near, first), (far, second), (far_near, first + second)):
+        owner = me + flip - 2 * (me & flip)
+        all_rows = lax.dynamic_update_index_in_dim(all_rows, block, owner, 0)
+    ordered = jnp.transpose(all_rows, (1, 2, 0, 3, 4, 5))
+    return ordered.reshape(step, -1, parts, level_count), near
+
+
+def orders(index):
+    return (1, 2) if index % 2 == 0 else (2, 1)
 
 
 def local(
@@ -51,15 +104,20 @@
     bases = []
     for i in range(chunks):
         part = slice(i * step, (i + 1) * step)
-        scaled = (coeffs[part].astype(jnp.float32) * spread).astype(jnp.bfloat16)
-        spectral_rows = jnp.einsum(
-            "mnj,mrkn->mjrk", legendre[part], scaled, preferred_element_type=jnp.float32
-        ).astype(jnp.bfloat16)
-        fields = jnp.einsum(
-            "mjrk,lk->mjrl", spectral_rows, mixing, preferred_element_type=jnp.float32
-        ).astype(jnp.bfloat16)
-        stacked = fields.reshape(step, band_count, local_rows, 2, level_count)
-        summed = lax.psum_scatter(stacked, "section", scatter_dimension=2, tiled=True)
+        halves = 2 if step % 2 == 0 else 1
+        sums = []
+        for h in range(halves):
+            begin = i * step + h * (step // halves)
+            sub = slice(begin, begin + step // halves)
+            scaled = (coeffs[sub].astype(jnp.float32) * spread).astype(jnp.bfloat16)
+            spectral_rows = jnp.einsum(
+                "mnj,mrkn->mjrk", legendre[sub], scaled, preferred_element_type=jnp.float32
+            ).astype(jnp.bfloat16)
+            fields = jnp.einsum(
+                "mjrk,lk->mjrl", spectral_rows, mixing, preferred_element_type=jnp.float32
+            ).astype(jnp.bfloat16)
+            sums.append(sum_rows(fields, band_count, *orders(h)))
+        summed = jnp.concatenate(sums, axis=0)
         moved = lax.all_to_all(summed, "band", split_axis=1, concat_axis=0, tiled=True)[:, 0]
         wave_ids = (
             jnp.arange(band_count, dtype=jnp.int32)[:, None] * wave_local
@@ -79,16 +137,19 @@
     adjoint_columns = ((own_weight * own_departures)[:, :, None] * wide_kernels).astype(jnp.bfloat16)
 
     pieces = []
+    nears = []
     for i in range(chunks):
         part = slice(i * step, (i + 1) * step)
         own_adjoint = jnp.einsum(
             "jqrm,jql->mjrl", bases[i], adjoint_columns, preferred_element_type=jnp.float32
         ).astype(jnp.bfloat16)
-        returned = lax.all_to_all(
-            own_adjoint[:, None], "band", split_axis=0, concat_axis=1, tiled=True
-        )
-        gathered = lax.all_gather(returned, "section", axis=2, tiled=True)
-        adjoint_all = gathered.reshape(step, row_count, 2, level_count)
+        by_band = own_adjoint.reshape(band_count, step, row_share, 2, level_count)
+        outgoing = jnp.swapaxes(by_band, 0, 1)
+        if i >= 2:
+            outgoing, _ = lax.optimization_barrier((outgoing, nears[i - 2]))
+        returned = lax.all_to_all(outgoing, "band", split_axis=1, concat_axis=1, tiled=True)
+        adjoint_all, near = gather_rows(returned, *orders(i))
+        nears.append(near)
         back_rows = jnp.einsum(
             "mjrl,lk->mjrk", adjoint_all, mixing, preferred_element_type=jnp.float32
         ).astype(jnp.bfloat16)

time: 604 us -> 584 us (0.967)
  blocking collectives: 127 us -> 15.5 us
  other arithmetic: 28.1 us -> 101 us
  matrix products: 195 us -> 145 us
  starting transfers between devices: 30.7 us -> 64.1 us
  waiting for transfers between devices: 131 us -> 160 us
  local copies, waits for them, and re-layouts: 67.3 us -> 86.3 us
  between operations: 14.5 us -> 1.46 us
    ppermute x0 -> x28, waiting for transfers between devices: none -> 117 us  [exchange(): return lax.ppermute(block, 'section', [(s, s ^ bit) for s in range(count)])]
    all_to_all x4 -> x0, blocking collectives: 116 us -> none  [local(): lax.all_to_all(own_adjoint[:, None], 'band', split_axis=0, concat_axis=1,...]
    reduce_scatter x4 -> x0, waiting for transfers between devices: 99.2 us -> none  [local(): lax.psum_scatter(stacked, 'section', scatter_dimension=2, tiled=True)]
    convert_element_type x0 -> x21, other arithmetic: none -> 67.5 us  [the longest x1 49.5 us: make_basis(): return (acc * (x * weight)).astype(jnp.bfloat16)]
    dot_general x4 -> x0, matrix products: 58.7 us -> none  [local(): jnp.einsum('jqrm,jql->mjrl', bases[i], adjoint_columns, preferred_element...]
    all_to_all x0 -> x4, waiting for transfers between devices: none -> 33.5 us  [local(): lax.all_to_all(outgoing, 'band', split_axis=1, concat_axis=1, tiled=True)]
    ppermute x0 -> x28, starting transfers between devices: none -> 30.4 us  [exchange(): return lax.ppermute(block, 'section', [(s, s ^ bit) for s in range(count)])]
    unnamed x0 -> x4, matrix products: none -> 28 us
  transfers between devices with their start and end apart: 12 -> 36, of which waited for: 7 -> 15; matrix products, arithmetic and copies ran while one was open for 35% -> 48% of each run, Pallas kernels for 0% -> 0%
where the time goes in v2:
time: 584 us; the launch traced here: 574 us
  waiting for transfers between devices  160 us (27%)
  matrix products  145 us (25%)
  other arithmetic  101 us (17%)
  local copies, waits for them, and re-layouts  86.3 us (15%)
  starting transfers between devices  64.1 us (11%)
  blocking collectives  15.5 us (3%)
    ppermute x28, waiting for transfers between devices, exchange(): return lax.ppermute(block, 'section', [(s, s ^ bit) for s in range(count)])  117 us
    convert_element_type x1, other arithmetic, make_basis(): return (acc * (x * weight)).astype(jnp.bfloat16)  49.5 us
    dot_general x8, matrix products, local(): jnp.einsum('mjrk,lk->mjrl', spectral_rows, mixing, preferred_element_type...  42.5 us
    dot_general x4, matrix products, local(): jnp.einsum('jqrm,mjrl->jql', basis, moved, preferred_element_type=jnp.flo...  38.1 us
    dot_general x4, matrix products, local(): jnp.einsum('mjrk,mnj->mrkn', back_rows, legendre[part], preferred_element...  37 us
    all_to_all x4, waiting for transfers between devices, local(): lax.all_to_all(outgoing, 'band', split_axis=1, concat_axis=1, tiled=True)  33.5 us
    ppermute x28, starting transfers between devices, exchange(): return lax.ppermute(block, 'section', [(s, s ^ bit) for s in range(count)])  30.4 us
    unnamed x4, matrix products  28 us
  transfers between devices with their start and end apart: 36, of which 15 were waited for; matrix products, arithmetic and copies ran while one was open for 48% of the time, Pallas kernels for 0%

profile of v2, /device:TPU:0, one launch (start us, length us, event | category | flops | bytes accessed | tf_op | source)
XLA Modules:
  0.0 574.4 jit_solution(2724860004962228576)
XLA Ops:
  60.3 13.2 %broadcast_multiply_fusion.3 = (f32[16,1024,128]{1,2,0:T(8,128)}, f32[16,1024,128]{1,2,0:T(8,128)}, f32[16,1024,128]{1,2,0:T(8,128)}, f32[16,1024,128]{1,2,0:T(8,128)}) fusion(f32[128]{0:T(128)S(1)} %convert_element_type.495, f32[16,1024]{1,0:T(8,128)S(1)} %convert_multiply_fusion.10, f32[128]{0:T(128)S(1)} %convert_element_type.527, ...), kind=kLoop, calls=%fused_computation.123 | loop fusion | flops 8388608 | bytes 33622016 | tf_op jit(solution)/shard_map/mul | solution.py:15
  122.0 37.1 %collective-permute-done.7 = bf16[8,8,16,2,128]{4,2,3,0,1:T(8,128)(2,1)S(1)} collective-permute-done((bf16[8,8,16,2,128]{4,2,3,0,1:T(8,128)(2,1)S(1)}, bf16[8,8,16,2,128]{4,2,3,0,1:T(8,128)(2,1)S(1)}, u32[]{:S(2)}, u32[]{:S(2)}) %collective-permute-start.7) | collective-permute-done | bytes 524320 | tf_op jit(solution)/shard_map/ppermute | solution.py:30
  175.8 7.4 %collective-permute-done.11 = bf16[8,8,16,2,128]{4,2,3,0,1:T(8,128)(2,1)S(1)} collective-permute-done((bf16[8,8,16,2,128]{4,2,3,0,1:T(8,128)(2,1)S(1)}, bf16[8,8,16,2,128]{4,2,3,0,1:T(8,128)(2,1)S(1)}, u32[]{:S(2)}, u32[]{:S(2)}) %collective-permute-start.11) | collective-permute-done | bytes 524320 | tf_op jit(solution)/shard_map/ppermute | solution.py:30
  197.1 49.5 %multiply_convert_fusion.3 = (bf16[16,1024,2,128]{1,3,2,0:T(8,128)(2,1)}, bf16[16,1024,2,128]{1,3,2,0:T(8,128)(2,1)}, bf16[16,1024,2,128]{1,3,2,0:T(8,128)(2,1)}, bf16[16,1024,2,128]{1,3,2,0:T(8,128)(2,1)}) fusion(f32[128]{0:T(128)S(1)} %select_n.228, f32[2]{0:T(128)S(1)} %convert_multiply_fusion.11, f32[16,1024,128]{1,2,0:T(8,128)} %get-tuple-element.24, ...), kind=kLoop, calls=%fused_computation.40 | loop fusion | flops 352321536 | bytes 67110920 | tf_op jit(solution)/shard_map/convert_element_type | solution.py:25
  251.2 6.4 %copy.175 = bf16[16,1024,128]{1,2,0:T(8,128)(2,1)} copy(bf16[16,1024,128]{2,1,0:T(8,128)(2,1)} %constant_dynamic-slice_fusion.16) | data formatting | bytes 8388608
  266.8 8.7 %fusion.323 = f32[16,1024,128,1]{1,2,3,0:T(8,128)} fusion(bf16[16,1024,2,128]{1,3,2,0:T(8,128)(2,1)} %get-tuple-element.28, bf16[128,16,2,128]{3,1,2,0:T(8,128)(2,1)S(1)} %bitcast.552), kind=kOutput, calls=%fused_computation.263 | convolution fusion | flops 1073741824 | bytes 17825792 | tf_op jit(solution)/shard_map/jqrm,mjrl->jql/dot_general | solution.py:129
  275.5 8.7 %fusion.321 = f32[16,1024,128,1]{1,2,3,0:T(8,128)} fusion(bf16[16,1024,2,128]{1,3,2,0:T(8,128)(2,1)} %get-tuple-element.29, bf16[128,16,2,128]{3,1,2,0:T(8,128)(2,1)S(1)} %bitcast.553), kind=kOutput, calls=%fused_computation.259 | convolution fusion | flops 1073741824 | bytes 17825792 | tf_op jit(solution)/shard_map/jqrm,mjrl->jql/dot_general | solution.py:129
  293.4 15.3 %fusion.24 = f32[16,1024]{1,0:T(8,128)S(1)} fusion(bf16[16,1024,128]{1,2,0:T(8,128)(2,1)} %copy.175, f32[16,1024,128,1]{1,2,3,0:T(8,128)} %fusion.319, f32[16,1024,128,1]{1,2,3,0:T(8,128)} %fusion.321, f32[16,1024,128,1]{1,2,3,0:T(8,128)} %fusion.323, bf16[16,1024,2,128]{1,3,2,0:T(8,128)(2,1)} %get-tuple-element.31, bf16[128,16,2,128]{3,1,2,0:T(8,128)(2,1)} %bitcast.96), kind=kOutput, calls=%fused_computation.51 | convolution fusion | flops 1086308352 | bytes 38862848 | tf_op jit(solution)/shard_map/jqrm,mjrl->jql/dot_general | solution.py:129
  309.7 7.0 %fusion.92 = f32[16,128,256]{1,2,0:S(1)} fusion(bf16[16,1024,256]{1,2,0:T(8,128)(2,1)} %bitcast.550, bf16[16,1024,128]{1,2,0:T(8,128)(2,1)} %copy.175, f32[16,1024]{1,0:T(8,128)S(1)} %get-tuple-element.6), kind=kOutput, calls=%fused_computation.131 | convolution fusion | flops 1080033280 | bytes 14745600
  322.6 7.0 %fusion.90 = f32[16,128,256]{1,2,0:S(1)} fusion(bf16[16,1024,256]{1,2,0:T(8,128)(2,1)} %bitcast.549, bf16[16,1024,128]{1,2,0:T(8,128)(2,1)} %copy.175, f32[16,1024]{1,0:T(8,128)S(1)} %get-tuple-element.6), kind=kOutput, calls=%fused_computation.130 | convolution fusion | flops 1080033280 | bytes 14745600
  331.4 17.7 %all-to-all-done.4 = bf16[16,8,16,2,128]{4,2,3,0,1:T(8,128)(2,1)S(1)} async-done(((bf16[16,8,16,2,128]{4,2,3,0,1:T(8,128)(2,1)}), bf16[16,8,16,2,128]{4,2,3,0,1:T(8,128)(2,1)S(1)}, u32[]{:S(2)}, u32[]{:S(2)}) %all-to-all-start.4) | async-done | bytes 1048608 | tf_op jit(solution)/shard_map/all_to_all | solution.py:150
  354.5 7.0 %fusion.88 = f32[16,128,256]{1,2,0:S(1)} fusion(bf16[16,1024,256]{1,2,0:T(8,128)(2,1)} %bitcast.546, bf16[16,1024,128]{1,2,0:T(8,128)(2,1)} %copy.175, f32[16,1024]{1,0:T(8,128)S(1)} %get-tuple-element.6), kind=kOutput, calls=%fused_computation.129 | convolution fusion | flops 1080033280 | bytes 14745600
  363.4 15.8 %all-to-all-done.5 = bf16[16,8,16,2,128]{4,2,3,0,1:T(8,128)(2,1)S(1)} async-done(((bf16[16,8,16,2,128]{4,2,3,0,1:T(8,128)(2,1)}), bf16[16,8,16,2,128]{4,2,3,0,1:T(8,128)(2,1)S(1)}, u32[]{:S(2)}, u32[]{:S(2)}) %all-to-all-start.5) | async-done | bytes 1048608 | tf_op jit(solution)/shard_map/all_to_all | solution.py:150
  384.5 7.0 %fusion.86 = f32[16,128,256]{1,2,0:S(1)} fusion(bf16[16,1024,256]{1,2,0:T(8,128)(2,1)} %bitcast.551, bf16[16,1024,128]{1,2,0:T(8,128)(2,1)} %copy.175, f32[16,1024]{1,0:T(8,128)S(1)} %get-tuple-element.6), kind=kOutput, calls=%fused_computation.128 | convolution fusion | flops 1080033280 | bytes 14745600
  393.3 15.5 %all_gather.3 = f32[64,1024]{1,0:T(8,128)S(1)} all-gather(f32[16,1024]{1,0:T(8,128)S(1)} %get-tuple-element.7), channel_id=1, replica_groups=mesh['section'=4,'band'=8] {'section'}, dimensions={0}, use_global_device_ids=true | all-gather | bytes 327680 | tf_op jit(solution)/shard_map/all_gather | solution.py:162
  423.3 11.9 %collective-permute-done.17 = bf16[16,8,16,2,128]{4,2,1,3,0:T(8,128)(2,1)S(1)} collective-permute-done((bf16[16,8,16,2,128]{4,2,1,3,0:T(8,128)(2,1)}, bf16[16,8,16,2,128]{4,2,1,3,0:T(8,128)(2,1)S(1)}, u32[]{:S(2)}, u32[]{:S(2)}) %collective-permute-start.17) | collective-permute-done | bytes 1048608 | tf_op jit(solution)/shard_map/ppermute | solution.py:30
  442.7 12.0 %collective-permute-done.18 = bf16[16,8,16,2,128]{4,2,1,3,0:T(8,128)(2,1)} collective-permute-done((bf16[16,8,16,2,128]{4,2,1,3,0:T(8,128)(2,1)}, bf16[16,8,16,2,128]{4,2,1,3,0:T(8,128)(2,1)}, u32[]{:S(2)}, u32[]{:S(2)}) %collective-permute-start.18) | collective-permute-done | bytes 1048608 | tf_op jit(solution)/shard_map/ppermute | solution.py:30
  458.5 9.2 %fusion.37 = bf16[16,2,128,512]{3,2,1,0:T(8,128)(2,1)} fusion(f32[512]{0:T(512)S(1)} %bitcast.583, bf16[1,64,2,128,512]{4,3,2,1,0:T(8,128)(2,1)} %param.9, bf16[64,512,512]{2,1,0:T(8,128)(2,1)} %param.10, bf16[16,512,2,128]{3,1,2,0:T(8,128)(2,1)} %bitcast.110, bf16[1,128,128]{2,1,0:T(8,128)(2,1)S(1)} %copy-done), kind=kOutput, calls=%fused_computation.68 | convolution fusion | flops 2694840320 | bytes 21006336 | tf_op jit(solution)/shard_map/mjrk,mnj->mrkn/dot_general | solution.py:156
  472.3 9.3 %fusion.34 = bf16[16,2,128,512]{3,2,1,0:T(8,128)(2,1)} fusion(bf16[1,64,2,128,512]{4,3,2,1,0:T(8,128)(2,1)} %param.9, f32[512]{0:T(512)S(1)} %bitcast.584, bf16[64,512,512]{2,1,0:T(8,128)(2,1)} %param.10, bf16[16,512,2,128]{3,1,2,0:T(8,128)(2,1)} %bitcast.559, bf16[1,128,128]{2,1,0:T(8,128)(2,1)S(1)} %copy-done), kind=kOutput, calls=%fused_computation.64 | convolution fusion | flops 2694840320 | bytes 21006336 | tf_op jit(solution)/shard_map/mjrk,mnj->mrkn/dot_general | solution.py:156
  502.4 18.1 %collective-permute-done.23 = bf16[16,8,16,2,128]{4,2,1,3,0:T(8,128)(2,1)S(1)} collective-permute-done((bf16[16,8,16,2,128]{4,2,1,3,0:T(8,128)(2,1)}, bf16[16,8,16,2,128]{4,2,1,3,0:T(8,128)(2,1)S(1)}, u32[]{:S(2)}, u32[]{:S(2)}) %collective-permute-start.23) | collective-permute-done | bytes 1048608 | tf_op jit(solution)/shard_map/ppermute | solution.py:30
  522.8 15.9 %collective-permute-done.24 = bf16[16,8,16,2,128]{4,2,1,3,0:T(8,128)(2,1)S(1)} collective-permute-done((bf16[16,8,16,2,128]{4,2,1,3,0:T(8,128)(2,1)S(1)}, bf16[16,8,16,2,128]{4,2,1,3,0:T(8,128)(2,1)S(1)}, u32[]{:S(2)}, u32[]{:S(2)}) %collective-permute-start.24) | collective-permute-done | bytes 1048608 | tf_op jit(solution)/shard_map/ppermute | solution.py:30
  539.9 9.3 %fusion.31 = bf16[16,2,128,512]{3,2,1,0:T(8,128)(2,1)} fusion(bf16[1,64,2,128,512]{4,3,2,1,0:T(8,128)(2,1)} %param.9, f32[512]{0:T(512)S(1)} %bitcast.585, bf16[64,512,512]{2,1,0:T(8,128)(2,1)} %param.10, bf16[16,512,2,128]{3,1,2,0:T(8,128)(2,1)} %bitcast.140, bf16[1,128,128]{2,1,0:T(8,128)(2,1)S(1)} %copy-done), kind=kOutput, calls=%fused_computation.60 | convolution fusion | flops 2694840320 | bytes 21006336 | tf_op jit(solution)/shard_map/mjrk,mnj->mrkn/dot_general | solution.py:156
  550.3 9.2 %fusion.28 = bf16[16,2,128,512]{3,2,1,0:T(8,128)(2,1)} fusion(bf16[1,64,2,128,512]{4,3,2,1,0:T(8,128)(2,1)} %param.9, f32[512]{0:T(512)S(1)} %bitcast.586, bf16[64,512,512]{2,1,0:T(8,128)(2,1)} %param.10, bf16[16,512,2,128]{3,1,2,0:T(8,128)(2,1)} %bitcast.155, bf16[1,128,128]{2,1,0:T(8,128)(2,1)S(1)} %copy-done), kind=kOutput, calls=%fused_computation.56 | convolution fusion | flops 2694840320 | bytes 21006336 | tf_op jit(solution)/shard_map/mjrk,mnj->mrkn/dot_general | solution.py:156
  559.5 14.0 %maximum_bitcast_fusion = bf16[1,64,2,128,512]{4,3,2,1,0:T(8,128)(2,1)} fusion(bf16[16,2,128,512]{3,2,1,0:T(8,128)(2,1)} %fusion.28, bf16[16,2,128,512]{3,2,1,0:T(8,128)(2,1)} %fusion.31, bf16[16,2,128,512]{3,2,1,0:T(8,128)(2,1)} %fusion.34, bf16[16,2,128,512]{3,2,1,0:T(8,128)(2,1)} %fusion.37), kind=kLoop, calls=%fused_computation.12 | loop fusion | flops 25165824 | bytes 33554432 | tf_op jit(solution)/shard_map/broadcast_in_dim | solution.py:163
  (196 shorter events, 240.7 us)
Async XLA Ops:
  7.8 80.2 %collective-permute-start.2 = (bf16[8,8,2,16,2,128]{5,3,4,0,1,2:T(8,128)(2,1)}, bf16[8,8,2,16,2,128]{5,3,4,0,1,2:T(8,128)(2,1)}, u32[]{:S(2)}, u32[]{:S(2)}) collective-permute-start(bf16[8,8,2,16,2,128]{5,3,4,0,1,2:T(8,128)(2,1)} %bitcast.544), channel_id=1, source_target_pairs={{0,16},{8,24},{16,0},{24,8},{1,17},{9,25},{17,1},{25,9},{2,18},{10... | collective-permute-start | bytes 3145736 | tf_op jit(solution)/shard_map/ppermute | solution.py:30
  18.2 73.2 %collective-permute-start = (bf16[8,8,2,16,2,128]{5,3,4,0,1,2:T(8,128)(2,1)}, bf16[8,8,2,16,2,128]{5,3,4,0,1,2:T(8,128)(2,1)}, u32[]{:S(2)}, u32[]{:S(2)}) collective-permute-start(bf16[8,8,2,16,2,128]{5,3,4,0,1,2:T(8,128)(2,1)} %bitcast.545), channel_id=1, source_target_pairs={{0,8},{8,0},{16,24},{24,16},{1,9},{9,1},{17,25},{25,17},{2,10},{10... | collective-permute-start | bytes 3145736 | tf_op jit(solution)/shard_map/ppermute | solution.py:30
  27.0 85.1 %collective-permute-start.6 = (bf16[8,8,2,16,2,128]{5,3,4,0,1,2:T(8,128)(2,1)}, bf16[8,8,2,16,2,128]{5,3,4,0,1,2:T(8,128)(2,1)}, u32[]{:S(2)}, u32[]{:S(2)}) collective-permute-start(bf16[8,8,2,16,2,128]{5,3,4,0,1,2:T(8,128)(2,1)} %bitcast.542), channel_id=1, source_target_pairs={{0,16},{8,24},{16,0},{24,8},{1,17},{9,25},{17,1},{25,9},{2,18},{10... | collective-permute-start | bytes 3145736 | tf_op jit(solution)/shard_map/ppermute | solution.py:30
  35.0 79.7 %collective-permute-start.4 = (bf16[8,8,2,16,2,128]{5,3,4,0,1,2:T(8,128)(2,1)}, bf16[8,8,2,16,2,128]{5,3,4,0,1,2:T(8,128)(2,1)}, u32[]{:S(2)}, u32[]{:S(2)}) collective-permute-start(bf16[8,8,2,16,2,128]{5,3,4,0,1,2:T(8,128)(2,1)} %bitcast.543), channel_id=1, source_target_pairs={{0,8},{8,0},{16,24},{24,16},{1,9},{9,1},{17,25},{25,17},{2,10},{10... | collective-permute-start | bytes 3145736 | tf_op jit(solution)/shard_map/ppermute | solution.py:30
  44.7 73.4 %collective-permute-start.14 = (bf16[8,8,2,16,2,128]{5,3,4,0,1,2:T(8,128)(2,1)}, bf16[8,8,2,16,2,128]{5,3,4,0,1,2:T(8,128)(2,1)}, u32[]{:S(2)}, u32[]{:S(2)}) collective-permute-start(bf16[8,8,2,16,2,128]{5,3,4,0,1,2:T(8,128)(2,1)} %bitcast.538), channel_id=1, source_target_pairs={{0,16},{8,24},{16,0},{24,8},{1,17},{9,25},{17,1},{25,9},{2,18},{10... | collective-permute-start | bytes 3145736 | tf_op jit(solution)/shard_map/ppermute | solution.py:30
  102.1 69.8 %collective-permute-start.12 = (bf16[8,8,2,16,2,128]{5,3,4,0,1,2:T(8,128)(2,1)}, bf16[8,8,2,16,2,128]{5,3,4,0,1,2:T(8,128)(2,1)}, u32[]{:S(2)}, u32[]{:S(2)}) collective-permute-start(bf16[8,8,2,16,2,128]{5,3,4,0,1,2:T(8,128)(2,1)} %bitcast.539), channel_id=1, source_target_pairs={{0,8},{8,0},{16,24},{24,16},{1,9},{9,1},{17,25},{25,17},{2,10},{10... | collective-permute-start | bytes 3145736 | tf_op jit(solution)/shard_map/ppermute | solution.py:30
  105.3 61.6 %collective-permute-start.10 = (bf16[8,8,2,16,2,128]{5,3,4,0,1,2:T(8,128)(2,1)}, bf16[8,8,2,16,2,128]{5,3,4,0,1,2:T(8,128)(2,1)}, u32[]{:S(2)}, u32[]{:S(2)}) collective-permute-start(bf16[8,8,2,16,2,128]{5,3,4,0,1,2:T(8,128)(2,1)} %bitcast.540), channel_id=1, source_target_pairs={{0,16},{8,24},{16,0},{24,8},{1,17},{9,25},{17,1},{25,9},{2,18},{10... | collective-permute-start | bytes 3145736 | tf_op jit(solution)/shard_map/ppermute | solution.py:30
  107.0 55.0 %all-to-all-start = ((bf16[16,8,16,2,128]{4,2,3,0,1:T(8,128)(2,1)}), bf16[16,8,16,2,128]{4,2,3,0,1:T(8,128)(2,1)S(1)}, u32[]{:S(2)}, u32[]{:S(2)}) async-start(bf16[16,8,16,2,128]{4,2,3,0,1:T(8,128)(2,1)} %pad_maximum_fusion), calls=%async_computation | async-start | bytes 2097152 | tf_op jit(solution)/shard_map/all_to_all | solution.py:121
  112.1 57.3 %collective-permute-start.8 = (bf16[8,8,2,16,2,128]{5,3,4,0,1,2:T(8,128)(2,1)}, bf16[8,8,2,16,2,128]{5,3,4,0,1,2:T(8,128)(2,1)}, u32[]{:S(2)}, u32[]{:S(2)}) collective-permute-start(bf16[8,8,2,16,2,128]{5,3,4,0,1,2:T(8,128)(2,1)} %bitcast.574), channel_id=1, source_target_pairs={{0,8},{8,0},{16,24},{24,16},{1,9},{9,1},{17,25},{25,17},{2,10},{10... | collective-permute-start | bytes 3145736 | tf_op jit(solution)/shard_map/ppermute | solution.py:30
  114.6 44.5 %collective-permute-start.7 = (bf16[8,8,16,2,128]{4,2,3,0,1:T(8,128)(2,1)S(1)}, bf16[8,8,16,2,128]{4,2,3,0,1:T(8,128)(2,1)S(1)}, u32[]{:S(2)}, u32[]{:S(2)}) collective-permute-start(bf16[8,8,16,2,128]{4,2,3,0,1:T(8,128)(2,1)S(1)} %dynamic-slice_bitcast_fusion.4), channel_id=1, source_target_pairs={{0,8},{8,0},{16,24},{24,16},{1,9},{9,1},{17,25},{25,17},{2,10},{10... | collective-permute-start | bytes 1572872 | tf_op jit(solution)/shard_map/ppermute | solution.py:30
  118.0 42.8 %collective-permute-start.5 = (bf16[8,8,16,2,128]{4,2,3,0,1:T(8,128)(2,1)S(1)}, bf16[8,8,16,2,128]{4,2,3,0,1:T(8,128)(2,1)S(1)}, u32[]{:S(2)}, u32[]{:S(2)}) collective-permute-start(bf16[8,8,16,2,128]{4,2,3,0,1:T(8,128)(2,1)S(1)} %dynamic-slice_bitcast_fusion.5), channel_id=1, source_target_pairs={{0,16},{8,24},{16,0},{24,8},{1,17},{9,25},{17,1},{25,9},{2,18},{10... | collective-permute-start | bytes 1572872 | tf_op jit(solution)/shard_map/ppermute | solution.py:30
  159.2 98.5 %collective-permute-start.15 = (bf16[8,8,16,2,128]{4,2,3,0,1:T(8,128)(2,1)}, bf16[8,8,16,2,128]{4,2,3,0,1:T(8,128)(2,1)}, u32[]{:S(2)}, u32[]{:S(2)}) collective-permute-start(bf16[8,8,16,2,128]{4,2,3,0,1:T(8,128)(2,1)} %dynamic-slice_bitcast_fusion), channel_id=1, source_target_pairs={{0,8},{8,0},{16,24},{24,16},{1,9},{9,1},{17,25},{25,17},{2,10},{10... | collective-permute-start | bytes 1572872 | tf_op jit(solution)/shard_map/ppermute | solution.py:30
  174.3 84.7 %collective-permute-start.13 = (bf16[8,8,16,2,128]{4,2,3,0,1:T(8,128)(2,1)}, bf16[8,8,16,2,128]{4,2,3,0,1:T(8,128)(2,1)}, u32[]{:S(2)}, u32[]{:S(2)}) collective-permute-start(bf16[8,8,16,2,128]{4,2,3,0,1:T(8,128)(2,1)} %dynamic-slice_bitcast_fusion.1), channel_id=1, source_target_pairs={{0,16},{8,24},{16,0},{24,8},{1,17},{9,25},{17,1},{25,9},{2,18},{10... | collective-permute-start | bytes 1572872 | tf_op jit(solution)/shard_map/ppermute | solution.py:30
  193.5 68.0 %all-to-all-start.2 = ((bf16[16,8,16,2,128]{4,2,3,0,1:T(8,128)(2,1)}), bf16[16,8,16,2,128]{4,2,3,0,1:T(8,128)(2,1)S(1)}, u32[]{:S(2)}, u32[]{:S(2)}) async-start(bf16[16,8,16,2,128]{4,2,3,0,1:T(8,128)(2,1)} %pad_maximum_fusion.2), calls=%async_computation.2 | async-start | bytes 2097152 | tf_op jit(solution)/shard_map/all_to_all | solution.py:121
  261.5 31.9 %all-to-all-start.3 = ((bf16[16,8,16,2,128]{4,2,3,0,1:T(8,128)(2,1)}), bf16[16,8,16,2,128]{4,2,3,0,1:T(8,128)(2,1)}, u32[]{:S(2)}, u32[]{:S(2)}) async-start(bf16[16,8,16,2,128]{4,2,3,0,1:T(8,128)(2,1)} %pad_maximum_fusion.3), calls=%async_computation.3 | async-start | bytes 2097152 | tf_op jit(solution)/shard_map/all_to_all | solution.py:121
  380.5 36.4 %collective-permute-start.19 = (bf16[16,8,16,2,128]{4,2,1,3,0:T(8,128)(2,1)}, bf16[16,8,16,2,128]{4,2,1,3,0:T(8,128)(2,1)}, u32[]{:S(2)}, u32[]{:S(2)}) collective-permute-start(bf16[16,8,16,2,128]{4,2,1,3,0:T(8,128)(2,1)} %copy.119), channel_id=1, source_target_pairs={{0,16},{8,24},{16,0},{24,8},{1,17},{9,25},{17,1},{25,9},{2,18},{10... | collective-permute-start | bytes 3145736 | tf_op jit(solution)/shard_map/ppermute | solution.py:30
  381.0 55.5 %all-to-all-start.6 = ((bf16[16,8,16,2,128]{4,2,3,0,1:T(8,128)(2,1)}), bf16[16,8,16,2,128]{4,2,3,0,1:T(8,128)(2,1)S(1)}, u32[]{:S(2)}, u32[]{:S(2)}) async-start(bf16[16,8,16,2,128]{4,2,3,0,1:T(8,128)(2,1)} %bitcast.561), calls=%async_computation.6 | async-start | bytes 2097152 | tf_op jit(solution)/shard_map/all_to_all | solution.py:150
  416.9 37.8 %collective-permute-start.18 = (bf16[16,8,16,2,128]{4,2,1,3,0:T(8,128)(2,1)}, bf16[16,8,16,2,128]{4,2,1,3,0:T(8,128)(2,1)}, u32[]{:S(2)}, u32[]{:S(2)}) collective-permute-start(bf16[16,8,16,2,128]{4,2,1,3,0:T(8,128)(2,1)} %collective-permute-done.16), channel_id=1, source_target_pairs={{0,16},{8,24},{16,0},{24,8},{1,17},{9,25},{17,1},{25,9},{2,18},{10... | collective-permute-start | bytes 3145736 | tf_op jit(solution)/shard_map/ppermute | solution.py:30
  418.4 39.0 %collective-permute-start.21 = (bf16[16,8,16,2,128]{4,2,1,3,0:T(8,128)(2,1)}, bf16[16,8,16,2,128]{4,2,1,3,0:T(8,128)(2,1)S(1)}, u32[]{:S(2)}, u32[]{:S(2)}) collective-permute-start(bf16[16,8,16,2,128]{4,2,1,3,0:T(8,128)(2,1)} %collective-permute-done.19), channel_id=1, source_target_pairs={{0,8},{8,0},{16,24},{24,16},{1,9},{9,1},{17,25},{25,17},{2,10},{10... | collective-permute-start | bytes 3145736 | tf_op jit(solution)/shard_map/ppermute | solution.py:30
  436.4 34.0 %all-to-all-start.7 = ((bf16[16,8,16,2,128]{4,2,3,0,1:T(8,128)(2,1)}), bf16[16,8,16,2,128]{4,2,3,0,1:T(8,128)(2,1)S(1)}, u32[]{:S(2)}, u32[]{:S(2)}) async-start(bf16[16,8,16,2,128]{4,2,3,0,1:T(8,128)(2,1)} %bitcast.560), calls=%async_computation.7 | async-start | bytes 2097152 | tf_op jit(solution)/shard_map/all_to_all | solution.py:150
  481.6 38.9 %collective-permute-start.23 = (bf16[16,8,16,2,128]{4,2,1,3,0:T(8,128)(2,1)}, bf16[16,8,16,2,128]{4,2,1,3,0:T(8,128)(2,1)S(1)}, u32[]{:S(2)}, u32[]{:S(2)}) collective-permute-start(bf16[16,8,16,2,128]{4,2,1,3,0:T(8,128)(2,1)} %copy.126), channel_id=1, source_target_pairs={{0,16},{8,24},{16,0},{24,8},{1,17},{9,25},{17,1},{25,9},{2,18},{10... | collective-permute-start | bytes 3145736 | tf_op jit(solution)/shard_map/ppermute | solution.py:30
  483.0 38.7 %collective-permute-start.26 = (bf16[16,8,16,2,128]{4,2,1,3,0:T(8,128)(2,1)}, bf16[16,8,16,2,128]{4,2,1,3,0:T(8,128)(2,1)S(1)}, u32[]{:S(2)}, u32[]{:S(2)}) collective-permute-start(bf16[16,8,16,2,128]{4,2,1,3,0:T(8,128)(2,1)} %copy.133), channel_id=1, source_target_pairs={{0,8},{8,0},{16,24},{24,16},{1,9},{9,1},{17,25},{25,17},{2,10},{10... | collective-permute-start | bytes 3145736 | tf_op jit(solution)/shard_map/ppermute | solution.py:30
  495.3 43.3 %collective-permute-start.24 = (bf16[16,8,16,2,128]{4,2,1,3,0:T(8,128)(2,1)S(1)}, bf16[16,8,16,2,128]{4,2,1,3,0:T(8,128)(2,1)S(1)}, u32[]{:S(2)}, u32[]{:S(2)}) collective-permute-start(bf16[16,8,16,2,128]{4,2,1,3,0:T(8,128)(2,1)S(1)} %collective-permute-done.22), channel_id=1, source_target_pairs={{0,16},{8,24},{16,0},{24,8},{1,17},{9,25},{17,1},{25,9},{2,18},{10... | collective-permute-start | bytes 3145736 | tf_op jit(solution)/shard_map/ppermute | solution.py:30
  498.1 51.1 %collective-permute-start.27 = (bf16[16,8,16,2,128]{4,2,1,3,0:T(8,128)(2,1)}, bf16[16,8,16,2,128]{4,2,1,3,0:T(8,128)(2,1)S(1)}, u32[]{:S(2)}, u32[]{:S(2)}) collective-permute-start(bf16[16,8,16,2,128]{4,2,1,3,0:T(8,128)(2,1)} %collective-permute-done.25), channel_id=1, source_target_pairs={{0,8},{8,0},{16,24},{24,16},{1,9},{9,1},{17,25},{25,17},{2,10},{10... | collective-permute-start | bytes 3145736 | tf_op jit(solution)/shard_map/ppermute | solution.py:30
  (23 other events, 427.3 us)

commit v3 on v2

--- a/solution.py
+++ b/solution.py
@@ -124,7 +124,8 @@
             + i * step
             + jnp.arange(step, dtype=jnp.int32)
         ).reshape(-1)
-        basis = make_basis(own_lon, wave_ids)
+        chunk_lon, moved = lax.optimization_barrier((own_lon, moved))
+        basis = make_basis(chunk_lon, wave_ids)
         bases.append(basis)
         columns = columns + jnp.einsum(
             "jqrm,mjrl->jql", basis, moved, preferred_element_type=jnp.float32

time: 584 us -> 608 us (1.041)
  waiting for transfers between devices: 160 us -> 185 us
    ppermute x28, waiting for transfers between devices: 117 us -> 130 us  [exchange(): return lax.ppermute(block, 'section', [(s, s ^ bit) for s in range(count)])]
    all_to_all x4, waiting for transfers between devices: 10 us -> 22 us  [local(): lax.all_to_all(summed, 'band', split_axis=1, concat_axis=0, tiled=True)]
    mul x1 -> x2, other arithmetic: 13.2 us -> 16.2 us  [make_basis(): (longitude.astype(jnp.float32) * (1.0 / NLON))[..., None, None] * waves]
  transfers between devices with their start and end apart: 36 -> 36, of which waited for: 15 -> 16; matrix products, arithmetic and copies ran while one was open for 48% -> 32% of each run, Pallas kernels for 0% -> 0%
where the time goes in v3:
time: 608 us; the launch traced here: 598 us
  waiting for transfers between devices  185 us (30%)
  matrix products  141 us (23%)
  other arithmetic  104 us (17%)
  local copies, waits for them, and re-layouts  87.2 us (14%)
  starting transfers between devices  62.7 us (10%)
  blocking collectives  16.9 us (3%)
    ppermute x28, waiting for transfers between devices, exchange(): return lax.ppermute(block, 'section', [(s, s ^ bit) for s in range(count)])  130 us
    convert_element_type x1, other arithmetic, make_basis(): return (acc * (x * weight)).astype(jnp.bfloat16)  49.5 us
    dot_general x8, matrix products, local(): jnp.einsum('mjrk,lk->mjrl', spectral_rows, mixing, preferred_element_type...  41.1 us
    dot_general x4, matrix products, local(): jnp.einsum('mjrk,mnj->mrkn', back_rows, legendre[part], preferred_element...  37 us
    dot_general x4, matrix products, local(): jnp.einsum('jqrm,mjrl->jql', basis, moved, preferred_element_type=jnp.flo...  34.6 us
    all_to_all x4, waiting for transfers between devices, local(): lax.all_to_all(outgoing, 'band', split_axis=1, concat_axis=1, tiled=True)  32.6 us
    ppermute x28, starting transfers between devices, exchange(): return lax.ppermute(block, 'section', [(s, s ^ bit) for s in range(count)])  29.9 us
    unnamed x4, matrix products  28 us
  transfers between devices with their start and end apart: 36, of which 16 were waited for; matrix products, arithmetic and copies ran while one was open for 32% of the time, Pallas kernels for 0%

profile of v3, /device:TPU:0, one launch (start us, length us, event | category | flops | bytes accessed | tf_op | source)
XLA Modules:
  0.0 597.6 jit_solution(16034722375423511075)
XLA Ops:
  70.7 27.9 %collective-permute-done.11 = bf16[8,8,16,2,128]{4,2,3,0,1:T(8,128)(2,1)S(1)} collective-permute-done((bf16[8,8,16,2,128]{4,2,3,0,1:T(8,128)(2,1)S(1)}, bf16[8,8,16,2,128]{4,2,3,0,1:T(8,128)(2,1)S(1)}, u32[]{:S(2)}, u32[]{:S(2)}) %collective-permute-start.11) | collective-permute-done | bytes 524320 | tf_op jit(solution)/shard_map/ppermute | solution.py:30
  123.2 10.6 %collective-permute-done.15 = bf16[8,8,16,2,128]{4,2,3,0,1:T(8,128)(2,1)} collective-permute-done((bf16[8,8,16,2,128]{4,2,3,0,1:T(8,128)(2,1)}, bf16[8,8,16,2,128]{4,2,3,0,1:T(8,128)(2,1)}, u32[]{:S(2)}, u32[]{:S(2)}) %collective-permute-start.15) | collective-permute-done | bytes 524320 | tf_op jit(solution)/shard_map/ppermute | solution.py:30
  149.9 18.2 %collective-permute-done.1 = bf16[8,8,16,2,128]{4,2,3,0,1:T(8,128)(2,1)S(1)} collective-permute-done((bf16[8,8,16,2,128]{4,2,3,0,1:T(8,128)(2,1)S(1)}, bf16[8,8,16,2,128]{4,2,3,0,1:T(8,128)(2,1)S(1)}, u32[]{:S(2)}, u32[]{:S(2)}) %collective-permute-start.1) | collective-permute-done | bytes 524320 | tf_op jit(solution)/shard_map/ppermute | solution.py:30
  180.2 10.3 %collective-permute-done.5 = bf16[8,8,16,2,128]{4,2,3,0,1:T(8,128)(2,1)S(1)} collective-permute-done((bf16[8,8,16,2,128]{4,2,3,0,1:T(8,128)(2,1)S(1)}, bf16[8,8,16,2,128]{4,2,3,0,1:T(8,128)(2,1)S(1)}, u32[]{:S(2)}, u32[]{:S(2)}) %collective-permute-start.5) | collective-permute-done | bytes 524320 | tf_op jit(solution)/shard_map/ppermute | solution.py:30
  193.9 7.1 %all-to-all-done = bf16[16,8,16,2,128]{4,2,3,0,1:T(8,128)(2,1)S(1)} async-done(((bf16[16,8,16,2,128]{4,2,3,0,1:T(8,128)(2,1)}), bf16[16,8,16,2,128]{4,2,3,0,1:T(8,128)(2,1)S(1)}, u32[]{:S(2)}, u32[]{:S(2)}) %all-to-all-start) | async-done | bytes 1048608 | tf_op jit(solution)/shard_map/all_to_all | solution.py:121
  216.6 14.5 %all-to-all-done.1 = bf16[16,8,16,2,128]{4,2,3,0,1:T(8,128)(2,1)S(1)} async-done(((bf16[16,8,16,2,128]{4,2,3,0,1:T(8,128)(2,1)}), bf16[16,8,16,2,128]{4,2,3,0,1:T(8,128)(2,1)S(1)}, u32[]{:S(2)}, u32[]{:S(2)}) %all-to-all-start.1) | async-done | bytes 1048608 | tf_op jit(solution)/shard_map/all_to_all | solution.py:121
  231.1 8.0 %broadcast_multiply_fusion = (f32[16,1024,128]{1,2,0:T(8,128)}, f32[16,1024,128]{1,2,0:T(8,128)}) fusion(f32[128]{0:T(128)S(1)} %convert_element_type.626, f32[16,1024]{1,0:T(8,128)S(1)} %convert_multiply_fusion.10, f32[128]{0:T(128)S(1)} %convert_element_type.594, f32[16,1024]{1,0:T(8,128)S(1)} %convert_multiply_fusion.11), kind=kLoop, calls=%fused_computation.112 | loop fusion | flops 4194304 | bytes 16909312 | tf_op jit(solution)/shard_map/mul | solution.py:15
  239.1 8.3 %broadcast_multiply_fusion.2 = (f32[16,1024,128]{1,2,0:T(8,128)}, f32[16,1024,128]{1,2,0:T(8,128)}) fusion(f32[128]{0:T(128)S(1)} %convert_element_type.562, f32[16,1024]{1,0:T(8,128)S(1)} %convert_multiply_fusion.12, f32[128]{0:T(128)S(1)} %convert_element_type.529, f32[16,1024]{1,0:T(8,128)S(1)} %convert_multiply_fusion.13), kind=kLoop, calls=%fused_computation.118 | loop fusion | flops 4194304 | bytes 16909312 | tf_op jit(solution)/shard_map/mul | solution.py:15
  247.3 49.5 %multiply_convert_fusion.3 = (bf16[16,1024,2,128]{1,3,2,0:T(8,128)(2,1)}, bf16[16,1024,2,128]{1,3,2,0:T(8,128)(2,1)}, bf16[16,1024,2,128]{1,3,2,0:T(8,128)(2,1)}, bf16[16,1024,2,128]{1,3,2,0:T(8,128)(2,1)}) fusion(f32[128]{0:T(128)S(1)} %select_n.235, f32[2]{0:T(128)S(1)} %convert_multiply_fusion.14, f32[16,1024,128]{1,2,0:T(8,128)} %get-tuple-element.51, ...), kind=kLoop, calls=%fused_computation.40 | loop fusion | flops 352321536 | bytes 67110920 | tf_op jit(solution)/shard_map/convert_element_type | solution.py:25
  296.9 8.8 %fusion.323 = f32[16,1024,128,1]{1,2,3,0:T(8,128)} fusion(bf16[16,1024,2,128]{1,3,2,0:T(8,128)(2,1)} %get-tuple-element.40, bf16[128,16,2,128]{3,1,2,0:T(8,128)(2,1)S(1)} %bitcast.553), kind=kOutput, calls=%fused_computation.263 | convolution fusion | flops 1073741824 | bytes 17825792 | tf_op jit(solution)/shard_map/jqrm,mjrl->jql/dot_general | solution.py:130
  316.1 15.3 %fusion.24 = f32[16,1024]{1,0:T(8,128)S(1)} fusion(bf16[16,1024,128]{1,2,0:T(8,128)(2,1)} %copy.175, f32[16,1024,128,1]{1,2,3,0:T(8,128)} %fusion.319, f32[16,1024,128,1]{1,2,3,0:T(8,128)} %fusion.321, f32[16,1024,128,1]{1,2,3,0:T(8,128)} %fusion.323, bf16[16,1024,2,128]{1,3,2,0:T(8,128)(2,1)} %get-tuple-element.43, bf16[128,16,2,128]{3,1,2,0:T(8,128)(2,1)} %bitcast.96), kind=kOutput, calls=%fused_computation.51 | convolution fusion | flops 1086308352 | bytes 38862848 | tf_op jit(solution)/shard_map/jqrm,mjrl->jql/dot_general | solution.py:130
  345.3 7.0 %fusion.90 = f32[16,128,256]{1,2,0:S(1)} fusion(bf16[16,1024,256]{1,2,0:T(8,128)(2,1)} %bitcast.549, bf16[16,1024,128]{1,2,0:T(8,128)(2,1)} %copy.175, f32[16,1024]{1,0:T(8,128)S(1)} %get-tuple-element.22), kind=kOutput, calls=%fused_computation.130 | convolution fusion | flops 1080033280 | bytes 14745600
  354.1 17.7 %all-to-all-done.4 = bf16[16,8,16,2,128]{4,2,3,0,1:T(8,128)(2,1)S(1)} async-done(((bf16[16,8,16,2,128]{4,2,3,0,1:T(8,128)(2,1)}), bf16[16,8,16,2,128]{4,2,3,0,1:T(8,128)(2,1)S(1)}, u32[]{:S(2)}, u32[]{:S(2)}) %all-to-all-start.4) | async-done | bytes 1048608 | tf_op jit(solution)/shard_map/all_to_all | solution.py:151
  387.0 14.9 %all-to-all-done.5 = bf16[16,8,16,2,128]{4,2,3,0,1:T(8,128)(2,1)S(1)} async-done(((bf16[16,8,16,2,128]{4,2,3,0,1:T(8,128)(2,1)}), bf16[16,8,16,2,128]{4,2,3,0,1:T(8,128)(2,1)S(1)}, u32[]{:S(2)}, u32[]{:S(2)}) %all-to-all-start.5) | async-done | bytes 1048608 | tf_op jit(solution)/shard_map/all_to_all | solution.py:151
  416.1 16.9 %all_gather.3 = f32[64,1024]{1,0:T(8,128)} all-gather(f32[16,1024]{1,0:T(8,128)S(1)} %get-tuple-element.23), channel_id=1, replica_groups=mesh['section'=4,'band'=8] {'section'}, dimensions={0}, use_global_device_ids=true | all-gather | bytes 327680 | tf_op jit(solution)/shard_map/all_gather | solution.py:163
  447.3 11.9 %collective-permute-done.17 = bf16[16,8,16,2,128]{4,2,1,3,0:T(8,128)(2,1)S(1)} collective-permute-done((bf16[16,8,16,2,128]{4,2,1,3,0:T(8,128)(2,1)}, bf16[16,8,16,2,128]{4,2,1,3,0:T(8,128)(2,1)S(1)}, u32[]{:S(2)}, u32[]{:S(2)}) %collective-permute-start.17) | collective-permute-done | bytes 1048608 | tf_op jit(solution)/shard_map/ppermute | solution.py:30
  466.7 11.9 %collective-permute-done.18 = bf16[16,8,16,2,128]{4,2,1,3,0:T(8,128)(2,1)} collective-permute-done((bf16[16,8,16,2,128]{4,2,1,3,0:T(8,128)(2,1)}, bf16[16,8,16,2,128]{4,2,1,3,0:T(8,128)(2,1)}, u32[]{:S(2)}, u32[]{:S(2)}) %collective-permute-start.18) | collective-permute-done | bytes 1048608 | tf_op jit(solution)/shard_map/ppermute | solution.py:30
  482.5 9.2 %fusion.37 = bf16[16,2,128,512]{3,2,1,0:T(8,128)(2,1)} fusion(f32[512]{0:T(512)S(1)} %bitcast.582, bf16[1,64,2,128,512]{4,3,2,1,0:T(8,128)(2,1)} %param.9, bf16[64,512,512]{2,1,0:T(8,128)(2,1)} %param.10, bf16[16,512,2,128]{3,1,2,0:T(8,128)(2,1)} %bitcast.110, bf16[1,128,128]{2,1,0:T(8,128)(2,1)S(1)} %copy-done.8), kind=kOutput, calls=%fused_computation.68 | convolution fusion | flops 2694840320 | bytes 21006336 | tf_op jit(solution)/shard_map/mjrk,mnj->mrkn/dot_general | solution.py:157
  496.2 9.3 %fusion.34 = bf16[16,2,128,512]{3,2,1,0:T(8,128)(2,1)} fusion(bf16[1,64,2,128,512]{4,3,2,1,0:T(8,128)(2,1)} %param.9, f32[512]{0:T(512)S(1)} %bitcast.583, bf16[64,512,512]{2,1,0:T(8,128)(2,1)} %param.10, bf16[16,512,2,128]{3,1,2,0:T(8,128)(2,1)} %bitcast.559, bf16[1,128,128]{2,1,0:T(8,128)(2,1)S(1)} %copy-done.8), kind=kOutput, calls=%fused_computation.64 | convolution fusion | flops 2694840320 | bytes 21006336 | tf_op jit(solution)/shard_map/mjrk,mnj->mrkn/dot_general | solution.py:157
  526.3 17.2 %collective-permute-done.23 = bf16[16,8,16,2,128]{4,2,1,3,0:T(8,128)(2,1)S(1)} collective-permute-done((bf16[16,8,16,2,128]{4,2,1,3,0:T(8,128)(2,1)}, bf16[16,8,16,2,128]{4,2,1,3,0:T(8,128)(2,1)S(1)}, u32[]{:S(2)}, u32[]{:S(2)}) %collective-permute-start.23) | collective-permute-done | bytes 1048608 | tf_op jit(solution)/shard_map/ppermute | solution.py:30
  545.8 16.0 %collective-permute-done.24 = bf16[16,8,16,2,128]{4,2,1,3,0:T(8,128)(2,1)S(1)} collective-permute-done((bf16[16,8,16,2,128]{4,2,1,3,0:T(8,128)(2,1)S(1)}, bf16[16,8,16,2,128]{4,2,1,3,0:T(8,128)(2,1)S(1)}, u32[]{:S(2)}, u32[]{:S(2)}) %collective-permute-start.24) | collective-permute-done | bytes 1048608 | tf_op jit(solution)/shard_map/ppermute | solution.py:30
  563.0 9.3 %fusion.31 = bf16[16,2,128,512]{3,2,1,0:T(8,128)(2,1)} fusion(bf16[1,64,2,128,512]{4,3,2,1,0:T(8,128)(2,1)} %param.9, f32[512]{0:T(512)S(1)} %bitcast.584, bf16[64,512,512]{2,1,0:T(8,128)(2,1)} %param.10, bf16[16,512,2,128]{3,1,2,0:T(8,128)(2,1)} %bitcast.140, bf16[1,128,128]{2,1,0:T(8,128)(2,1)S(1)} %copy-done.8), kind=kOutput, calls=%fused_computation.60 | convolution fusion | flops 2694840320 | bytes 21006336 | tf_op jit(solution)/shard_map/mjrk,mnj->mrkn/dot_general | solution.py:157
  573.5 9.2 %fusion.28 = bf16[16,2,128,512]{3,2,1,0:T(8,128)(2,1)} fusion(bf16[1,64,2,128,512]{4,3,2,1,0:T(8,128)(2,1)} %param.9, f32[512]{0:T(512)S(1)} %bitcast.585, bf16[64,512,512]{2,1,0:T(8,128)(2,1)} %param.10, bf16[16,512,2,128]{3,1,2,0:T(8,128)(2,1)} %bitcast.155, bf16[1,128,128]{2,1,0:T(8,128)(2,1)S(1)} %copy-done.8), kind=kOutput, calls=%fused_computation.56 | convolution fusion | flops 2694840320 | bytes 21006336 | tf_op jit(solution)/shard_map/mjrk,mnj->mrkn/dot_general | solution.py:157
  582.7 14.0 %maximum_bitcast_fusion = bf16[1,64,2,128,512]{4,3,2,1,0:T(8,128)(2,1)} fusion(bf16[16,2,128,512]{3,2,1,0:T(8,128)(2,1)} %fusion.28, bf16[16,2,128,512]{3,2,1,0:T(8,128)(2,1)} %fusion.31, bf16[16,2,128,512]{3,2,1,0:T(8,128)(2,1)} %fusion.34, bf16[16,2,128,512]{3,2,1,0:T(8,128)(2,1)} %fusion.37), kind=kLoop, calls=%fused_computation.12 | loop fusion | flops 25165824 | bytes 33554432 | tf_op jit(solution)/shard_map/broadcast_in_dim | solution.py:164
  (205 shorter events, 253.2 us)
Async XLA Ops:
  7.2 55.6 %collective-permute-start.10 = (bf16[8,8,2,16,2,128]{5,3,4,0,1,2:T(8,128)(2,1)}, bf16[8,8,2,16,2,128]{5,3,4,0,1,2:T(8,128)(2,1)}, u32[]{:S(2)}, u32[]{:S(2)}) collective-permute-start(bf16[8,8,2,16,2,128]{5,3,4,0,1,2:T(8,128)(2,1)} %bitcast.540), channel_id=1, source_target_pairs={{0,16},{8,24},{16,0},{24,8},{1,17},{9,25},{17,1},{25,9},{2,18},{10... | collective-permute-start | bytes 3145736 | tf_op jit(solution)/shard_map/ppermute | solution.py:30
  17.6 48.3 %collective-permute-start.8 = (bf16[8,8,2,16,2,128]{5,3,4,0,1,2:T(8,128)(2,1)}, bf16[8,8,2,16,2,128]{5,3,4,0,1,2:T(8,128)(2,1)}, u32[]{:S(2)}, u32[]{:S(2)}) collective-permute-start(bf16[8,8,2,16,2,128]{5,3,4,0,1,2:T(8,128)(2,1)} %bitcast.541), channel_id=1, source_target_pairs={{0,8},{8,0},{16,24},{24,16},{1,9},{9,1},{17,25},{25,17},{2,10},{10... | collective-permute-start | bytes 3145736 | tf_op jit(solution)/shard_map/ppermute | solution.py:30
  26.5 41.6 %collective-permute-start.14 = (bf16[8,8,2,16,2,128]{5,3,4,0,1,2:T(8,128)(2,1)}, bf16[8,8,2,16,2,128]{5,3,4,0,1,2:T(8,128)(2,1)}, u32[]{:S(2)}, u32[]{:S(2)}) collective-permute-start(bf16[8,8,2,16,2,128]{5,3,4,0,1,2:T(8,128)(2,1)} %bitcast.538), channel_id=1, source_target_pairs={{0,16},{8,24},{16,0},{24,8},{1,17},{9,25},{17,1},{25,9},{2,18},{10... | collective-permute-start | bytes 3145736 | tf_op jit(solution)/shard_map/ppermute | solution.py:30
  34.4 74.4 %collective-permute-start.12 = (bf16[8,8,2,16,2,128]{5,3,4,0,1,2:T(8,128)(2,1)}, bf16[8,8,2,16,2,128]{5,3,4,0,1,2:T(8,128)(2,1)}, u32[]{:S(2)}, u32[]{:S(2)}) collective-permute-start(bf16[8,8,2,16,2,128]{5,3,4,0,1,2:T(8,128)(2,1)} %bitcast.539), channel_id=1, source_target_pairs={{0,8},{8,0},{16,24},{24,16},{1,9},{9,1},{17,25},{25,17},{2,10},{10... | collective-permute-start | bytes 3145736 | tf_op jit(solution)/shard_map/ppermute | solution.py:30
  42.3 101.0 %collective-permute-start = (bf16[8,8,2,16,2,128]{5,3,4,0,1,2:T(8,128)(2,1)}, bf16[8,8,2,16,2,128]{5,3,4,0,1,2:T(8,128)(2,1)}, u32[]{:S(2)}, u32[]{:S(2)}) collective-permute-start(bf16[8,8,2,16,2,128]{5,3,4,0,1,2:T(8,128)(2,1)} %bitcast.545), channel_id=1, source_target_pairs={{0,8},{8,0},{16,24},{24,16},{1,9},{9,1},{17,25},{25,17},{2,10},{10... | collective-permute-start | bytes 3145736 | tf_op jit(solution)/shard_map/ppermute | solution.py:30
  62.8 83.9 %collective-permute-start.2 = (bf16[8,8,2,16,2,128]{5,3,4,0,1,2:T(8,128)(2,1)}, bf16[8,8,2,16,2,128]{5,3,4,0,1,2:T(8,128)(2,1)}, u32[]{:S(2)}, u32[]{:S(2)}) collective-permute-start(bf16[8,8,2,16,2,128]{5,3,4,0,1,2:T(8,128)(2,1)} %bitcast.544), channel_id=1, source_target_pairs={{0,16},{8,24},{16,0},{24,8},{1,17},{9,25},{17,1},{25,9},{2,18},{10... | collective-permute-start | bytes 3145736 | tf_op jit(solution)/shard_map/ppermute | solution.py:30
  65.9 32.7 %collective-permute-start.11 = (bf16[8,8,16,2,128]{4,2,3,0,1:T(8,128)(2,1)S(1)}, bf16[8,8,16,2,128]{4,2,3,0,1:T(8,128)(2,1)S(1)}, u32[]{:S(2)}, u32[]{:S(2)}) collective-permute-start(bf16[8,8,16,2,128]{4,2,3,0,1:T(8,128)(2,1)S(1)} %dynamic-slice_bitcast_fusion.2), channel_id=1, source_target_pairs={{0,8},{8,0},{16,24},{24,16},{1,9},{9,1},{17,25},{25,17},{2,10},{10... | collective-permute-start | bytes 1572872 | tf_op jit(solution)/shard_map/ppermute | solution.py:30
  68.1 32.1 %collective-permute-start.9 = (bf16[8,8,16,2,128]{4,2,3,0,1:T(8,128)(2,1)S(1)}, bf16[8,8,16,2,128]{4,2,3,0,1:T(8,128)(2,1)S(1)}, u32[]{:S(2)}, u32[]{:S(2)}) collective-permute-start(bf16[8,8,16,2,128]{4,2,3,0,1:T(8,128)(2,1)S(1)} %dynamic-slice_bitcast_fusion.3), channel_id=1, source_target_pairs={{0,16},{8,24},{16,0},{24,8},{1,17},{9,25},{17,1},{25,9},{2,18},{10... | collective-permute-start | bytes 1572872 | tf_op jit(solution)/shard_map/ppermute | solution.py:30
  98.6 75.9 %collective-permute-start.4 = (bf16[8,8,2,16,2,128]{5,3,4,0,1,2:T(8,128)(2,1)}, bf16[8,8,2,16,2,128]{5,3,4,0,1,2:T(8,128)(2,1)}, u32[]{:S(2)}, u32[]{:S(2)}) collective-permute-start(bf16[8,8,2,16,2,128]{5,3,4,0,1,2:T(8,128)(2,1)} %bitcast.543), channel_id=1, source_target_pairs={{0,8},{8,0},{16,24},{24,16},{1,9},{9,1},{17,25},{25,17},{2,10},{10... | collective-permute-start | bytes 3145736 | tf_op jit(solution)/shard_map/ppermute | solution.py:30
  101.5 36.7 %all-to-all-start.2 = ((bf16[16,8,16,2,128]{4,2,3,0,1:T(8,128)(2,1)}), bf16[16,8,16,2,128]{4,2,3,0,1:T(8,128)(2,1)S(1)}, u32[]{:S(2)}, u32[]{:S(2)}) async-start(bf16[16,8,16,2,128]{4,2,3,0,1:T(8,128)(2,1)} %pad_maximum_fusion.2), calls=%async_computation.2 | async-start | bytes 2097152 | tf_op jit(solution)/shard_map/all_to_all | solution.py:121
  133.8 42.8 %collective-permute-start.6 = (bf16[8,8,2,16,2,128]{5,3,4,0,1,2:T(8,128)(2,1)}, bf16[8,8,2,16,2,128]{5,3,4,0,1,2:T(8,128)(2,1)}, u32[]{:S(2)}, u32[]{:S(2)}) collective-permute-start(bf16[8,8,2,16,2,128]{5,3,4,0,1,2:T(8,128)(2,1)} %bitcast.542), channel_id=1, source_target_pairs={{0,16},{8,24},{16,0},{24,8},{1,17},{9,25},{17,1},{25,9},{2,18},{10... | collective-permute-start | bytes 3145736 | tf_op jit(solution)/shard_map/ppermute | solution.py:30
  138.2 31.7 %all-to-all-start.3 = ((bf16[16,8,16,2,128]{4,2,3,0,1:T(8,128)(2,1)}), bf16[16,8,16,2,128]{4,2,3,0,1:T(8,128)(2,1)}, u32[]{:S(2)}, u32[]{:S(2)}) async-start(bf16[16,8,16,2,128]{4,2,3,0,1:T(8,128)(2,1)} %pad_maximum_fusion.3), calls=%async_computation.3 | async-start | bytes 2097152 | tf_op jit(solution)/shard_map/all_to_all | solution.py:121
  169.9 31.1 %all-to-all-start = ((bf16[16,8,16,2,128]{4,2,3,0,1:T(8,128)(2,1)}), bf16[16,8,16,2,128]{4,2,3,0,1:T(8,128)(2,1)S(1)}, u32[]{:S(2)}, u32[]{:S(2)}) async-start(bf16[16,8,16,2,128]{4,2,3,0,1:T(8,128)(2,1)} %pad_maximum_fusion), calls=%async_computation | async-start | bytes 2097152 | tf_op jit(solution)/shard_map/all_to_all | solution.py:121
  341.2 30.5 %all-to-all-start.4 = ((bf16[16,8,16,2,128]{4,2,3,0,1:T(8,128)(2,1)}), bf16[16,8,16,2,128]{4,2,3,0,1:T(8,128)(2,1)S(1)}, u32[]{:S(2)}, u32[]{:S(2)}) async-start(bf16[16,8,16,2,128]{4,2,3,0,1:T(8,128)(2,1)} %bitcast.537), calls=%async_computation.4 | async-start | bytes 2097152 | tf_op jit(solution)/shard_map/all_to_all | solution.py:151
  403.2 37.7 %collective-permute-start.19 = (bf16[16,8,16,2,128]{4,2,1,3,0:T(8,128)(2,1)}, bf16[16,8,16,2,128]{4,2,1,3,0:T(8,128)(2,1)}, u32[]{:S(2)}, u32[]{:S(2)}) collective-permute-start(bf16[16,8,16,2,128]{4,2,1,3,0:T(8,128)(2,1)} %copy.119), channel_id=1, source_target_pairs={{0,16},{8,24},{16,0},{24,8},{1,17},{9,25},{17,1},{25,9},{2,18},{10... | collective-permute-start | bytes 3145736 | tf_op jit(solution)/shard_map/ppermute | solution.py:30
  403.7 56.8 %all-to-all-start.6 = ((bf16[16,8,16,2,128]{4,2,3,0,1:T(8,128)(2,1)}), bf16[16,8,16,2,128]{4,2,3,0,1:T(8,128)(2,1)S(1)}, u32[]{:S(2)}, u32[]{:S(2)}) async-start(bf16[16,8,16,2,128]{4,2,3,0,1:T(8,128)(2,1)} %bitcast.561), calls=%async_computation.6 | async-start | bytes 2097152 | tf_op jit(solution)/shard_map/all_to_all | solution.py:151
  433.5 30.7 %collective-permute-start.20 = (bf16[16,8,16,2,128]{4,2,1,3,0:T(8,128)(2,1)}, bf16[16,8,16,2,128]{4,2,1,3,0:T(8,128)(2,1)}, u32[]{:S(2)}, u32[]{:S(2)}) collective-permute-start(bf16[16,8,16,2,128]{4,2,1,3,0:T(8,128)(2,1)} %copy.119), channel_id=1, source_target_pairs={{0,8},{8,0},{16,24},{24,16},{1,9},{9,1},{17,25},{25,17},{2,10},{10... | collective-permute-start | bytes 3145736 | tf_op jit(solution)/shard_map/ppermute | solution.py:30
  440.9 37.7 %collective-permute-start.18 = (bf16[16,8,16,2,128]{4,2,1,3,0:T(8,128)(2,1)}, bf16[16,8,16,2,128]{4,2,1,3,0:T(8,128)(2,1)}, u32[]{:S(2)}, u32[]{:S(2)}) collective-permute-start(bf16[16,8,16,2,128]{4,2,1,3,0:T(8,128)(2,1)} %collective-permute-done.16), channel_id=1, source_target_pairs={{0,16},{8,24},{16,0},{24,8},{1,17},{9,25},{17,1},{25,9},{2,18},{10... | collective-permute-start | bytes 3145736 | tf_op jit(solution)/shard_map/ppermute | solution.py:30
  441.5 39.8 %collective-permute-start.21 = (bf16[16,8,16,2,128]{4,2,1,3,0:T(8,128)(2,1)}, bf16[16,8,16,2,128]{4,2,1,3,0:T(8,128)(2,1)S(1)}, u32[]{:S(2)}, u32[]{:S(2)}) collective-permute-start(bf16[16,8,16,2,128]{4,2,1,3,0:T(8,128)(2,1)} %collective-permute-done.19), channel_id=1, source_target_pairs={{0,8},{8,0},{16,24},{24,16},{1,9},{9,1},{17,25},{25,17},{2,10},{10... | collective-permute-start | bytes 3145736 | tf_op jit(solution)/shard_map/ppermute | solution.py:30
  460.5 33.0 %all-to-all-start.7 = ((bf16[16,8,16,2,128]{4,2,3,0,1:T(8,128)(2,1)}), bf16[16,8,16,2,128]{4,2,3,0,1:T(8,128)(2,1)S(1)}, u32[]{:S(2)}, u32[]{:S(2)}) async-start(bf16[16,8,16,2,128]{4,2,3,0,1:T(8,128)(2,1)} %bitcast.560), calls=%async_computation.7 | async-start | bytes 2097152 | tf_op jit(solution)/shard_map/all_to_all | solution.py:151
  505.5 38.0 %collective-permute-start.23 = (bf16[16,8,16,2,128]{4,2,1,3,0:T(8,128)(2,1)}, bf16[16,8,16,2,128]{4,2,1,3,0:T(8,128)(2,1)S(1)}, u32[]{:S(2)}, u32[]{:S(2)}) collective-permute-start(bf16[16,8,16,2,128]{4,2,1,3,0:T(8,128)(2,1)} %copy.126), channel_id=1, source_target_pairs={{0,16},{8,24},{16,0},{24,8},{1,17},{9,25},{17,1},{25,9},{2,18},{10... | collective-permute-start | bytes 3145736 | tf_op jit(solution)/shard_map/ppermute | solution.py:30
  506.0 38.7 %collective-permute-start.26 = (bf16[16,8,16,2,128]{4,2,1,3,0:T(8,128)(2,1)}, bf16[16,8,16,2,128]{4,2,1,3,0:T(8,128)(2,1)S(1)}, u32[]{:S(2)}, u32[]{:S(2)}) collective-permute-start(bf16[16,8,16,2,128]{4,2,1,3,0:T(8,128)(2,1)} %copy.133), channel_id=1, source_target_pairs={{0,8},{8,0},{16,24},{24,16},{1,9},{9,1},{17,25},{25,17},{2,10},{10... | collective-permute-start | bytes 3145736 | tf_op jit(solution)/shard_map/ppermute | solution.py:30
  519.3 42.6 %collective-permute-start.24 = (bf16[16,8,16,2,128]{4,2,1,3,0:T(8,128)(2,1)S(1)}, bf16[16,8,16,2,128]{4,2,1,3,0:T(8,128)(2,1)S(1)}, u32[]{:S(2)}, u32[]{:S(2)}) collective-permute-start(bf16[16,8,16,2,128]{4,2,1,3,0:T(8,128)(2,1)S(1)} %collective-permute-done.22), channel_id=1, source_target_pairs={{0,16},{8,24},{16,0},{24,8},{1,17},{9,25},{17,1},{25,9},{2,18},{10... | collective-permute-start | bytes 3145736 | tf_op jit(solution)/shard_map/ppermute | solution.py:30
  521.1 51.2 %collective-permute-start.27 = (bf16[16,8,16,2,128]{4,2,1,3,0:T(8,128)(2,1)}, bf16[16,8,16,2,128]{4,2,1,3,0:T(8,128)(2,1)S(1)}, u32[]{:S(2)}, u32[]{:S(2)}) collective-permute-start(bf16[16,8,16,2,128]{4,2,1,3,0:T(8,128)(2,1)} %collective-permute-done.25), channel_id=1, source_target_pairs={{0,8},{8,0},{16,24},{24,16},{1,9},{9,1},{17,25},{25,17},{2,10},{10... | collective-permute-start | bytes 3145736 | tf_op jit(solution)/shard_map/ppermute | solution.py:30
  (25 other events, 622.2 us)
